TPU v7x, 32 devices: a whole 2x2x4 slice. The times are simulated.
32 devices in a mesh: row: 4 (over z), col: 8 (over y, x, core).
Axes of the slice: x: 2, y: 2, z: 4, core: 2. Of those that a mesh axis runs over, the one named last changes fastest.
Arguments:
- nodes: bfloat16 [16384, 512], P(('row', 'col')), may hold values from -6 to 6
- cotangent: bfloat16 [16384, 512], P(('row', 'col')), may hold values from -6 to 6
- edge_source: int32 [65536], P(('row', 'col')), may hold values from 0 to 639
- edge_target: int32 [65536], P(('row', 'col')), may hold values from 0 to 511
- halo_lists: int32 [32, 4, 32], P(('row', 'col')), may hold values from 0 to 511
- pool_owner: int32 [16384], P(('row', 'col')), may hold values from 0 to 31, as said below
- pool_table: int32 [32, 1024], P(('row', 'col')), may hold values from -1 to 127, as said below
- source_weight: bfloat16 [512, 512], replicated, may hold values from -0.25 to 0.25
- target_weight: bfloat16 [512, 512], replicated, may hold values from -0.25 to 0.25
- edge_weight: bfloat16 [512, 512], replicated, may hold values from -0.25 to 0.25
- inner_weight: bfloat16 [1024, 512], replicated, may hold values from -0.1875 to 0.1875
- outer_weight: bfloat16 [512, 512], replicated, may hold values from -0.25 to 0.25
- coarse_weight: bfloat16 [512, 512], replicated, may hold values from -0.5 to 0.5
Outputs:
- updated: bfloat16 [16384, 512], P(('row', 'col'))
- node_gradient: float32 [16384, 512], P(('row', 'col'))
- source_gradient: float32 [512, 512], replicated
- target_gradient: float32 [512, 512], replicated
- edge_gradient: float32 [512, 512], replicated
- inner_gradient: float32 [1024, 512], replicated
- outer_gradient: float32 [512, 512], replicated
- coarse_gradient: float32 [512, 512], replicated
Inputs may be any that keep to these rules, and one draw needn't show every extreme that they name: `edge_source`: rows below 512 are the partition's own nodes; row 512 + k * 32 + j is row j of halo block k. `pool_owner`: at most 32 nodes of one partition name the same owner; one owner is named by exactly 32 nodes of every partition. `pool_table`: entry [o, q * 32 + k] is the coarse row of owner o for the node of rank k among the nodes of partition q that name o, and -1 where q names o fewer than k + 1 times.
All inputs are finite; a program needn't handle non-finite values.
Results may differ from a plain program's by a relative error of at most 0.014.
Values may be sent and summed in bfloat16 or wider, within the bound.
A program may use at most 128 MiB of HBM per device.

v0:
```python
import math

import jax
import jax.numpy as jnp
from jax import lax
from jax.sharding import PartitionSpec as P


def passed_along(value, axis, steps):
    count = lax.axis_size(axis)
    initial, last = (max(0, -steps), min(count, count - steps))
    return lax.ppermute(value, axis, [(source, source + steps) for source in range(initial, last)])


def product(first, second):
    return jnp.dot(first, second, preferred_element_type=jnp.float32)


def left_product(first, second):
    return lax.dot_general(
        first, second, (((0,), (0,)), ((), ())), preferred_element_type=jnp.float32
    )


def right_product(first, second):
    return lax.dot_general(
        first, second, (((1,), (1,)), ((), ())), preferred_element_type=jnp.float32
    )


def silu_slope(value):
    sigma = jax.nn.sigmoid(value)
    return sigma * (1.0 + value * (1.0 - sigma))


def trade_halo(blocks, flip):
    moved = []
    for number, offset in enumerate((1, -1)):
        moved.append(passed_along(blocks[number], "row", offset * flip))
    for number, offset in enumerate((1, -1)):
        moved.append(passed_along(blocks[2 + number], "col", offset * flip))
    return moved


def trade_slots(buffer):
    return lax.all_to_all(buffer, ("row", "col"), split_axis=0, concat_axis=0, tiled=True)


def toward_owners(values, slot, devices, capacity, trader):
    width = values.shape[1]
    outgoing = jnp.zeros((devices * capacity, width), values.dtype).at[slot].set(values)
    arrived = trader(outgoing.reshape(devices, capacity, width))
    return arrived.reshape(devices * capacity, width)


def toward_sources(coarse_values, table, slot, devices, capacity, trader):
    width = coarse_values.shape[1]
    picked = jnp.take(coarse_values, jnp.maximum(table, 0), axis=0)
    picked = jnp.where((table >= 0)[:, None], picked, jnp.zeros_like(picked))
    returned = trader(picked.reshape(devices, capacity, width)).reshape(devices * capacity, width)
    return jnp.take(returned, slot, axis=0)


def local(
    nodes,
    cotangent,
    edge_source,
    edge_target,
    halo_lists,
    pool_owner,
    pool_table,
    source_weight,
    target_weight,
    edge_weight,
    inner_weight,
    outer_weight,
    coarse_weight,
):
    devices = lax.axis_size("row") * lax.axis_size("col")
    count_rows, width = nodes.shape
    lists = halo_lists[0]
    halo_rows = lists.shape[1]
    table = pool_table[0]
    capacity = table.shape[0] // devices
    coarse_rows = count_rows // 4
    scale = 1.0 / math.sqrt(count_rows * devices)
    received = trade_halo([jnp.take(nodes, lists[number], axis=0) for number in range(4)], 1)
    extended = jnp.concatenate([nodes] + received, axis=0)
    source_side = product(extended, source_weight)
    target_side = product(nodes, target_weight)
    edge_linear = jnp.take(source_side, edge_source, axis=0) + jnp.take(
        target_side, edge_target, axis=0
    )
    edge_hidden = jax.nn.silu(edge_linear).astype(jnp.bfloat16)
    message_linear = product(edge_hidden, edge_weight)
    aggregate = jax.ops.segment_sum(jax.nn.silu(message_linear), edge_target, count_rows).astype(
        jnp.bfloat16
    )
    joined = jnp.concatenate([nodes, aggregate], axis=1)
    node_linear = product(joined, inner_weight)
    node_hidden = jax.nn.silu(node_linear).astype(jnp.bfloat16)
    refined = (nodes.astype(jnp.float32) + product(node_hidden, outer_weight)).astype(jnp.bfloat16)
    owner_hot = (pool_owner[:, None] == jnp.arange(devices, dtype=jnp.int32)[None, :]).astype(
        jnp.bfloat16
    )
    positions = jnp.arange(count_rows, dtype=jnp.int32)
    lower = (positions[:, None] > positions[None, :]).astype(jnp.bfloat16)
    rank = jnp.sum(product(lower, owner_hot) * owner_hot, axis=1).astype(jnp.int32)
    slot = pool_owner * capacity + rank
    member = (jnp.arange(coarse_rows, dtype=jnp.int32)[:, None] == table[None, :]).astype(
        jnp.bfloat16
    )
    count = jnp.maximum(jnp.sum(member, axis=1, dtype=jnp.float32), 1.0)[:, None]
    arrived = toward_owners(refined, slot, devices, capacity, trade_slots)
    coarse = (product(member, arrived) / count).astype(jnp.bfloat16)
    coarse_linear = product(coarse, coarse_weight)
    coarse_update = jax.nn.silu(coarse_linear).astype(jnp.bfloat16)
    parent_rows = toward_sources(coarse_update, table, slot, devices, capacity, trade_slots)
    arrived_grad = toward_owners(cotangent, slot, devices, capacity, trade_slots)
    grad_coarse = (product(member, arrived_grad) * silu_slope(coarse_linear)).astype(jnp.bfloat16)
    coarse_share = (right_product(grad_coarse, coarse_weight) / count).astype(jnp.bfloat16)
    share_rows = toward_sources(coarse_share, table, slot, devices, capacity, trade_slots)
    updated = (refined.astype(jnp.float32) + parent_rows.astype(jnp.float32)).astype(jnp.bfloat16)
    coarse_gradient = left_product(coarse, grad_coarse)
    grad_refined = cotangent.astype(jnp.float32) + share_rows.astype(jnp.float32)
    refined_low = grad_refined.astype(jnp.bfloat16)
    outer_gradient = left_product(node_hidden, refined_low)
    grad_hidden = (right_product(refined_low, outer_weight) * silu_slope(node_linear)).astype(
        jnp.bfloat16
    )
    inner_gradient = left_product(joined, grad_hidden)
    grad_joined = right_product(grad_hidden, inner_weight)
    grad_aggregate = grad_joined[:, width:].astype(jnp.bfloat16)
    grad_message = (
        jnp.take(grad_aggregate, edge_target, axis=0) * silu_slope(message_linear)
    ).astype(jnp.bfloat16)
    edge_gradient = left_product(edge_hidden, grad_message)
    grad_edges = right_product(grad_message, edge_weight) * silu_slope(edge_linear)
    grad_sources = jax.ops.segment_sum(grad_edges, edge_source, extended.shape[0]).astype(
        jnp.bfloat16
    )
    grad_targets = jax.ops.segment_sum(grad_edges, edge_target, count_rows).astype(jnp.bfloat16)
    source_gradient = left_product(extended, grad_sources)
    target_gradient = left_product(nodes, grad_targets)
    (
        source_gradient,
        target_gradient,
        edge_gradient,
        inner_gradient,
        outer_gradient,
        coarse_gradient,
    ) = lax.psum(
        (
            source_gradient,
            target_gradient,
            edge_gradient,
            inner_gradient,
            outer_gradient,
            coarse_gradient,
        ),
        ("row", "col"),
    )
    grad_extended = right_product(grad_sources, source_weight)
    back_blocks = grad_extended[count_rows:].astype(jnp.bfloat16).reshape(4, halo_rows, width)
    returned = trade_halo([back_blocks[number] for number in range(4)], -1)
    node_gradient = (
        grad_refined
        + grad_joined[:, :width]
        + right_product(grad_targets, target_weight)
        + grad_extended[:count_rows]
    )
    node_gradient = node_gradient.at[lists.reshape(-1)].add(
        jnp.concatenate(returned, axis=0).astype(jnp.float32)
    )
    return (
        updated,
        node_gradient,
        source_gradient * scale,
        target_gradient * scale,
        edge_gradient * scale,
        inner_gradient * scale,
        outer_gradient * scale,
        coarse_gradient * scale,
    )


def solution(mesh):
    in_specs = (
        P(("row", "col"), None),
        P(("row", "col"), None),
        P(("row", "col")),
        P(("row", "col")),
        P(("row", "col"), None, None),
        P(("row", "col")),
        P(("row", "col"), None),
        P(),
        P(),
        P(),
        P(),
        P(),
        P(),
    )
    out_specs = (P(("row", "col"), None), P(("row", "col"), None), P(), P(), P(), P(), P(), P())
    return jax.shard_map(local, mesh=mesh, in_specs=in_specs, out_specs=out_specs, check_vma=False)
```

profile of v0, /device:TPU:0, one launch (start us, length us, event | category | flops | bytes accessed | tf_op | source)
XLA Modules:
  0.0 463.1 jit_solution(3420387355164975699)
XLA Ops:
  8.1 1.7 gather_fusion.3
  9.9 4.9 %collective-permute-start = (bf16[32,512]{1,0:T(8,128)(2,1)S(1)}, bf16[32,512]{1,0:T(8,128)(2,1)S(1)}, u32[]{:S(2)}, u32[]{:S(2)}) collective-permute-start(bf16[32,512]{1,0:T(8,128)(2,1)S(1)} %broadcast_select_fusion.4), channel_id=1, source_target_pairs={{0,8},{8,16},{16,24},{1,9},{9,17},{17,25},{2,10},{10,18},{18,26},{... | collective-permute-start | bytes 98312 | tf_op jit(solution)/shard_map/ppermute | solution.py:12
  14.8 1.7 gather_fusion.4
  16.7 1.3 collective-permute-start.1
  18.0 1.7 gather_fusion.5
  19.8 1.5 collective-permute-start.2
  21.3 1.7 gather_fusion.6
  23.1 1.3 collective-permute-start.3
  25.1 1.3 compare_and_fusion
  26.4 1.6 fusion.53
  29.1 1.3 compare_and_fusion.2
  30.4 8.9 %gather_fusion.1 = f32[2048,512]{1,0:T(8,128)} fusion(f32[512,512]{1,0:T(8,128)S(1)} %fusion.53, s32[2048]{0:T(1024)S(1)} %get-tuple-element.46), kind=kCustom, calls=%fused_computation.9 | custom fusion | bytes 8396800 | tf_op jit(solution)/shard_map/jit(_take)/gather | solution.py:91
  39.4 1.5 fusion.52
  41.0 9.0 %gather_fusion = f32[2048,512]{1,0:T(8,128)} fusion(f32[640,512]{1,0:T(8,128)S(1)} %fusion.52, s32[2048]{0:T(1024)S(1)} %get-tuple-element.45), kind=kCustom, calls=%fused_computation.8 | custom fusion | bytes 8396800 | tf_op jit(solution)/shard_map/jit(_take)/gather | solution.py:91
  49.9 4.2 multiply_convert_fusion.1
  54.2 1.3 copy-done.5
  55.5 3.3 fusion.54
  58.8 14.6 %scatter_custom_fusion = f32[512,512]{1,0:T(8,128)S(1)} fusion(s32[2048]{0:T(1024)} %param.22, f32[2048,512]{1,0:T(8,128)} %fusion.54, f32[]{:T(128)} %constant.62.clone.1, f32[]{:T(128)} %constant.52.clone.1), kind=kCustom, calls=%fused_computation.19 | custom fusion | flops 5242880 | bytes 5243904 | tf_op jit(solution)/shard_map/scatter-add | solution.py:96
  75.5 3.6 scatter_custom_fusion.1
  79.1 9.9 %all-to-all-start = ((bf16[32,32,512]{2,1,0:T(8,128)(2,1)}), bf16[32,32,512]{2,1,0:T(8,128)(2,1)S(1)}, u32[]{:S(2)}, u32[]{:S(2)}) async-start(bf16[32,32,512]{2,1,0:T(8,128)(2,1)} %bitcast.5), calls=%async_computation | async-start | bytes 2097152 | tf_op jit(solution)/shard_map/all_to_all | solution.py:46
  89.1 4.0 scatter_custom_fusion.2
  93.0 22.1 %all-to-all-done = bf16[32,32,512]{2,1,0:T(8,128)(2,1)S(1)} async-done(((bf16[32,32,512]{2,1,0:T(8,128)(2,1)}), bf16[32,32,512]{2,1,0:T(8,128)(2,1)S(1)}, u32[]{:S(2)}, u32[]{:S(2)}) %all-to-all-start) | async-done | bytes 1048608 | tf_op jit(solution)/shard_map/all_to_all | solution.py:46
  115.1 3.7 all-to-all-start.2
  119.9 1.4 multiply_convert_fusion.3
  121.3 23.8 %all-to-all-done.2 = bf16[32,32,512]{2,1,0:T(8,128)(2,1)} async-done(((bf16[32,32,512]{2,1,0:T(8,128)(2,1)}), bf16[32,32,512]{2,1,0:T(8,128)(2,1)}, u32[]{:S(2)}, u32[]{:S(2)}) %all-to-all-start.2) | async-done | bytes 1048608 | tf_op jit(solution)/shard_map/all_to_all | solution.py:46
  145.1 1.5 fusion.8
  147.3 1.3 fusion.6
  148.7 4.0 gather_fusion.9
  152.6 5.1 %gather_fusion.7 = bf16[1024,512]{1,0:T(8,128)(2,1)} fusion(bf16[128,512]{1,0:T(8,128)(2,1)S(1)} %get-tuple-element.41, s32[1024]{0:T(1024)S(1)} %maximum_clamp_fusion), kind=kCustom, calls=%fused_computation.1.clone | custom fusion | bytes 2101248 | tf_op jit(solution)/shard_map/jit(_take)/gather | solution.py:58
  157.7 2.9 select_select_fusion
  160.6 3.6 all-to-all-start.3
  164.3 2.3 fusion.57
  166.6 23.9 %all-to-all-done.3 = bf16[32,32,512]{2,1,0:T(8,128)(2,1)S(1)} async-done(((bf16[32,32,512]{2,1,0:T(8,128)(2,1)}), bf16[32,32,512]{2,1,0:T(8,128)(2,1)S(1)}, u32[]{:S(2)}, u32[]{:S(2)}) %all-to-all-start.3) | async-done | bytes 1048608 | tf_op jit(solution)/shard_map/all_to_all | solution.py:46
  190.5 2.6 gather_fusion.10
  193.1 2.4 fusion.5
  196.3 1.3 copy-done.8
  197.7 9.2 %gather_fusion.2 = bf16[2048,512]{1,0:T(8,128)(2,1)} fusion(bf16[512,512]{1,0:T(8,128)(2,1)S(1)} %slice.97, s32[2048]{0:T(1024)S(1)} %get-tuple-element.46), kind=kCustom, calls=%fused_computation.10 | custom fusion | bytes 4202496 | tf_op jit(solution)/shard_map/jit(_take)/gather | solution.py:135
  206.9 3.8 multiply_convert_fusion
  210.7 1.3 copy-done.10
  213.0 4.3 multiply_multiply_fusion
  217.2 13.6 %scatter_custom_fusion.4 = f32[640,512]{1,0:T(8,128)S(1)} fusion(s32[2048]{0:T(1024)} %param.21, f32[2048,512]{1,0:T(8,128)} %multiply_multiply_fusion, f32[]{:T(128)} %constant.52.clone.1), kind=kCustom, calls=%fused_computation.55 | custom fusion | flops 1048576 | bytes 1311232 | tf_op jit(solution)/shard_map/scatter-add | solution.py:139
  230.8 13.7 %scatter_custom_fusion.3 = f32[512,512]{1,0:T(8,128)S(1)} fusion(s32[2048]{0:T(1024)} %param.22, f32[2048,512]{1,0:T(8,128)} %multiply_multiply_fusion, f32[]{:T(128)} %constant.52.clone.1), kind=kCustom, calls=%fused_computation.69 | custom fusion | flops 1048576 | bytes 1049088 | tf_op jit(solution)/shard_map/scatter-add | solution.py:142
  244.6 4.9 %fusion.56 = f32[512,512]{1,0:T(8,128)} fusion(bf16[2048,512]{1,0:T(8,128)(2,1)} %copy-done.5, bf16[2048,512]{1,0:T(8,128)(2,1)} %copy-done.10), kind=kOutput, calls=%fused_computation.140 | convolution fusion | flops 1073741824 | bytes 5242880 | tf_op jit(solution)/shard_map/dot_general | solution.py:20
  249.5 2.1 fusion.11
  251.6 1.7 fusion.47
  253.2 1.6 fusion.23
  254.8 1.5 convolution_bitcast_fusion
  256.3 3.6 all-to-all-start.1
  260.0 36.9 %all-to-all-done.1 = bf16[32,32,512]{2,1,0:T(8,128)(2,1)S(1)} async-done(((bf16[32,32,512]{2,1,0:T(8,128)(2,1)}), bf16[32,32,512]{2,1,0:T(8,128)(2,1)S(1)}, u32[]{:S(2)}, u32[]{:S(2)}) %all-to-all-start.1) | async-done | bytes 1048608 | tf_op jit(solution)/shard_map/all_to_all | solution.py:46
  297.0 2.0 gather_fusion.8
  299.0 1.7 fusion.51
  300.7 3.1 collective-permute-start.7
  303.9 1.3 collective-permute-start.6
  305.2 1.9 collective-permute-start.5
  307.1 1.3 collective-permute-start.4
  308.4 1.6 fusion.3
  311.1 2.4 collective-permute-done.4
  313.5 1.8 scatter_custom_fusion.5
  315.2 131.4 %all-reduce.3.cloned.1.call-done = (f32[512,512]{1,0:T(8,128)}, f32[512,512]{1,0:T(8,128)}, f32[512,512]{1,0:T(8,128)}, f32[1024,512]{1,0:T(8,128)}, f32[512,512]{1,0:T(8,128)}, /*index=5*/f32[512,512]{1,0:T(8,128)}) async-done(((f32[512,512]{1,0:T(8,128)}, f32[512,512]{1,0:T(8,128)}, f32[512,512]{1,0:T(8,128)}, f32[1024,512]{1,0:T(8,128)}, f32[512,512]{1,0:T(8,128)}, /*index=5*/f32[512,512]{1,0:T(8,128)}), ...) | async-done | bytes 7340048 | tf_op jit(solution)/shard_map/psum | solution.py:152
  446.7 2.4 broadcast_multiply_fusion.5
  449.1 2.4 broadcast_multiply_fusion.4
  452.6 1.5 broadcast_multiply_fusion
  454.1 1.1 broadcast_multiply_fusion.2
  455.2 1.1 broadcast_multiply_fusion.1
  (124 shorter events, 11.0 us)
Async XLA Ops:
  7.2 66.3 %copy-start = (bf16[1024,512]{1,0:T(8,128)(2,1)S(1)}, bf16[1024,512]{1,0:T(8,128)(2,1)}, u32[]{:S(2)}) copy-start(bf16[1024,512]{1,0:T(8,128)(2,1)} %param.29) | copy-start | bytes 3145732
  7.2 23.2 %copy-start.4 = (bf16[512,512]{1,0:T(8,128)(2,1)S(1)}, bf16[512,512]{1,0:T(8,128)(2,1)}, u32[]{:S(2)}) copy-start(bf16[512,512]{1,0:T(8,128)(2,1)} %param.19) | copy-start | bytes 1572868
  9.9 29.4 %collective-permute-start = (bf16[32,512]{1,0:T(8,128)(2,1)S(1)}, bf16[32,512]{1,0:T(8,128)(2,1)S(1)}, u32[]{:S(2)}, u32[]{:S(2)}) collective-permute-start(bf16[32,512]{1,0:T(8,128)(2,1)S(1)} %broadcast_select_fusion.4), channel_id=1, source_target_pairs={{0,8},{8,16},{16,24},{1,9},{9,17},{17,25},{2,10},{10,18},{18,26},{... | collective-permute-start | bytes 98312 | tf_op jit(solution)/shard_map/ppermute | solution.py:12
  16.7 22.7 %collective-permute-start.1 = (bf16[32,512]{1,0:T(8,128)(2,1)S(1)}, bf16[32,512]{1,0:T(8,128)(2,1)S(1)}, u32[]{:S(2)}, u32[]{:S(2)}) collective-permute-start(bf16[32,512]{1,0:T(8,128)(2,1)S(1)} %broadcast_select_fusion.3), channel_id=1, source_target_pairs={{8,0},{16,8},{24,16},{9,1},{17,9},{25,17},{10,2},{18,10},{26,18},{... | collective-permute-start | bytes 98312 | tf_op jit(solution)/shard_map/ppermute | solution.py:12
  19.8 19.6 %collective-permute-start.2 = (bf16[32,512]{1,0:T(8,128)(2,1)S(1)}, bf16[32,512]{1,0:T(8,128)(2,1)S(1)}, u32[]{:S(2)}, u32[]{:S(2)}) collective-permute-start(bf16[32,512]{1,0:T(8,128)(2,1)S(1)} %broadcast_select_fusion.2), channel_id=1, source_target_pairs={{0,1},{1,2},{2,3},{3,4},{4,5},{5,6},{6,7},{8,9},{9,10},{10,11},{11... | collective-permute-start | bytes 98312 | tf_op jit(solution)/shard_map/ppermute | solution.py:12
  23.1 16.3 %collective-permute-start.3 = (bf16[32,512]{1,0:T(8,128)(2,1)S(1)}, bf16[32,512]{1,0:T(8,128)(2,1)S(1)}, u32[]{:S(2)}, u32[]{:S(2)}) collective-permute-start(bf16[32,512]{1,0:T(8,128)(2,1)S(1)} %broadcast_select_fusion.1), channel_id=1, source_target_pairs={{1,0},{2,1},{3,2},{4,3},{5,4},{6,5},{7,6},{9,8},{10,9},{11,10},{12... | collective-permute-start | bytes 98312 | tf_op jit(solution)/shard_map/ppermute | solution.py:12
  49.9 5.6 %copy-start.19 = (bf16[512,512]{1,0:T(8,128)(2,1)S(1)}, bf16[512,512]{1,0:T(8,128)(2,1)}, u32[]{:S(2)}) copy-start(bf16[512,512]{1,0:T(8,128)(2,1)} %param.28) | copy-start | bytes 1572868
  54.2 1.3 copy-start.5
  73.4 1.2 copy-start.39
  73.5 1.5 copy-start.22
  74.6 1.0 copy-start.41
  75.5 3.6 copy-start.26
  75.5 43.3 %copy-start.30 = (s32[1,1024]{1,0:T(1,128)S(1)}, s32[1,1024]{1,0:T(1,128)}, u32[]{:S(2)}) copy-start(s32[1,1024]{1,0:T(1,128)} %param.25) | copy-start | bytes 12292
  79.1 36.0 %all-to-all-start = ((bf16[32,32,512]{2,1,0:T(8,128)(2,1)}), bf16[32,32,512]{2,1,0:T(8,128)(2,1)S(1)}, u32[]{:S(2)}, u32[]{:S(2)}) async-start(bf16[32,32,512]{2,1,0:T(8,128)(2,1)} %bitcast.5), calls=%async_computation | async-start | bytes 2097152 | tf_op jit(solution)/shard_map/all_to_all | solution.py:46
  115.1 30.0 %all-to-all-start.2 = ((bf16[32,32,512]{2,1,0:T(8,128)(2,1)}), bf16[32,32,512]{2,1,0:T(8,128)(2,1)}, u32[]{:S(2)}, u32[]{:S(2)}) async-start(bf16[32,32,512]{2,1,0:T(8,128)(2,1)} %bitcast.9), calls=%async_computation.2 | async-start | bytes 2097152 | tf_op jit(solution)/shard_map/all_to_all | solution.py:46
  119.0 26.1 %copy-start.40 = (f32[128]{0:T(128)}, f32[128]{0:T(128)S(1)}, u32[]{:S(2)}) copy-start(f32[128]{0:T(128)S(1)} %broadcast_maximum_fusion) | copy-start | bytes 1540
  119.9 26.7 %copy-start.28 = (bf16[128,512]{1,0:T(8,128)(2,1)}, bf16[128,512]{1,0:T(8,128)(2,1)S(1)}, u32[]{:S(2)}) copy-start(bf16[128,512]{1,0:T(8,128)(2,1)S(1)} %fusion.7) | copy-start | bytes 393220
  146.6 0.7 copy-start.29
  152.6 5.1 %copy-start.37 = (pred[1024]{0:T(1024)(128)(4,1)S(1)}, pred[1024]{0:T(1024)(128)(4,1)}, u32[]{:S(2)}) copy-start(pred[1024]{0:T(1024)(128)(4,1)} %get-tuple-element.31) | copy-start | bytes 3076
  152.6 5.1 %copy-start.38 = (pred[1024]{0:T(1024)(128)(4,1)S(1)}, pred[1024]{0:T(1024)(128)(4,1)}, u32[]{:S(2)}) copy-start(pred[1024]{0:T(1024)(128)(4,1)} %get-tuple-element.32) | copy-start | bytes 3076
  157.7 6.6 %copy-start.34 = (s32[512]{0:T(512)S(1)}, s32[512]{0:T(512)}, u32[]{:S(2)}) copy-start(s32[512]{0:T(512)} %get-tuple-element.18) | copy-start | bytes 6148
  160.6 32.5 %copy-start.35 = (pred[512]{0:T(512)(128)(4,1)S(1)}, pred[512]{0:T(512)(128)(4,1)}, u32[]{:S(2)}) copy-start(pred[512]{0:T(512)(128)(4,1)} %get-tuple-element.17) | copy-start | bytes 1540
  160.6 29.9 %all-to-all-start.3 = ((bf16[32,32,512]{2,1,0:T(8,128)(2,1)}), bf16[32,32,512]{2,1,0:T(8,128)(2,1)S(1)}, u32[]{:S(2)}, u32[]{:S(2)}) async-start(bf16[32,32,512]{2,1,0:T(8,128)(2,1)} %bitcast.56), calls=%async_computation.3 | async-start | bytes 2097152 | tf_op jit(solution)/shard_map/all_to_all | solution.py:46
  164.2 282.4 %all-reduce.3.cloned.1.call-start = ((), (), s32[]{:S(2)}) async-start(), calls=%async_computation.4 | async-start | bytes 14680064 | tf_op jit(solution)/shard_map/psum | solution.py:152
  195.5 11.4 %copy-start.24 = (bf16[512,512]{1,0:T(8,128)(2,1)}, bf16[512,512]{1,0:T(8,128)(2,1)S(1)}, u32[]{:S(2)}) copy-start(bf16[512,512]{1,0:T(8,128)(2,1)S(1)} %fusion.5) | copy-start | bytes 1572868
  196.2 1.3 copy-start.8
  197.6 9.2 %copy-start.31 = (pred[2048]{0:T(1024)(128)(4,1)S(1)}, pred[2048]{0:T(1024)(128)(4,1)}, u32[]{:S(2)}) copy-start(pred[2048]{0:T(1024)(128)(4,1)} %get-tuple-element.47) | copy-start | bytes 6148
  197.7 14.4 %copy-start.20 = (bf16[512,512]{1,0:T(8,128)(2,1)S(1)}, bf16[512,512]{1,0:T(8,128)(2,1)}, u32[]{:S(2)}) copy-start(bf16[512,512]{1,0:T(8,128)(2,1)} %param.28) | copy-start | bytes 1572868
  206.9 5.2 %copy-start.2 = (f32[2048,512]{1,0:T(8,128)S(1)}, f32[2048,512]{1,0:T(8,128)}, u32[]{:S(2)}) copy-start(f32[2048,512]{1,0:T(8,128)} %gather_fusion.1) | copy-start | bytes 12582916
  206.9 6.1 %copy-start.3 = (f32[2048,512]{1,0:T(8,128)S(1)}, f32[2048,512]{1,0:T(8,128)}, u32[]{:S(2)}) copy-start(f32[2048,512]{1,0:T(8,128)} %gather_fusion) | copy-start | bytes 12582916
  206.9 6.1 %copy-start.32 = (pred[2048]{0:T(1024)(128)(4,1)S(1)}, pred[2048]{0:T(1024)(128)(4,1)}, u32[]{:S(2)}) copy-start(pred[2048]{0:T(1024)(128)(4,1)} %get-tuple-element.48) | copy-start | bytes 6148
  210.7 1.3 copy-start.10
  244.5 10.3 %copy-start.6 = (f32[512,512]{1,0:T(8,128)}, f32[512,512]{1,0:T(8,128)S(1)}, u32[]{:S(2)}) copy-start(f32[512,512]{1,0:T(8,128)S(1)} %scatter_custom_fusion.3) | copy-start | bytes 3145732
  244.5 5.0 %copy-start.23 = (bf16[512,512]{1,0:T(8,128)(2,1)S(1)}, bf16[512,512]{1,0:T(8,128)(2,1)}, u32[]{:S(2)}) copy-start(bf16[512,512]{1,0:T(8,128)(2,1)} %copy-done.22) | copy-start | bytes 1572868
  244.5 4.9 %copy-start.25 = (bf16[512,512]{1,0:T(8,128)(2,1)S(1)}, bf16[512,512]{1,0:T(8,128)(2,1)}, u32[]{:S(2)}) copy-start(bf16[512,512]{1,0:T(8,128)(2,1)} %copy-done.24) | copy-start | bytes 1572868
  244.6 7.0 %copy-start.11 = (bf16[512,512]{1,0:T(8,128)(2,1)S(1)}, bf16[512,512]{1,0:T(8,128)(2,1)}, u32[]{:S(2)}) copy-start(bf16[512,512]{1,0:T(8,128)(2,1)} %gather_fusion.10) | copy-start | bytes 1572868
  244.6 7.0 %copy-start.21 = (bf16[512,512]{1,0:T(8,128)(2,1)S(1)}, bf16[512,512]{1,0:T(8,128)(2,1)}, u32[]{:S(2)}) copy-start(bf16[512,512]{1,0:T(8,128)(2,1)} %param.20) | copy-start | bytes 1572868
  244.6 7.0 %copy-start.36 = (pred[512]{0:T(512)(128)(4,1)S(1)}, pred[512]{0:T(512)(128)(4,1)}, u32[]{:S(2)}) copy-start(pred[512]{0:T(512)(128)(4,1)} %get-tuple-element.17) | copy-start | bytes 1540
  244.6 7.0 %copy-start.42 = (f32[512,512]{1,0:T(8,128)S(1)}, f32[512,512]{1,0:T(8,128)}, u32[]{:S(2)}) copy-start(f32[512,512]{1,0:T(8,128)} %copy-done.41) | copy-start | bytes 3145732
  256.3 3.7 copy-start.33
  256.3 40.7 %all-to-all-start.1 = ((bf16[32,32,512]{2,1,0:T(8,128)(2,1)}), bf16[32,32,512]{2,1,0:T(8,128)(2,1)S(1)}, u32[]{:S(2)}, u32[]{:S(2)}) async-start(bf16[32,32,512]{2,1,0:T(8,128)(2,1)} %bitcast.55), calls=%async_computation.1 | async-start | bytes 2097152 | tf_op jit(solution)/shard_map/all_to_all | solution.py:46
  297.0 11.4 %copy-start.12 = (bf16[512,512]{1,0:T(8,128)(2,1)S(1)}, bf16[512,512]{1,0:T(8,128)(2,1)}, u32[]{:S(2)}) copy-start(bf16[512,512]{1,0:T(8,128)(2,1)} %gather_fusion.10) | copy-start | bytes 1572868
  298.9 9.4 %copy-start.7 = (f32[512,512]{1,0:T(8,128)S(1)}, f32[512,512]{1,0:T(8,128)}, u32[]{:S(2)}) copy-start(f32[512,512]{1,0:T(8,128)} %copy-done.6) | copy-start | bytes 3145732
  298.9 9.4 %copy-start.9 = (f32[512,1024]{1,0:T(8,128)S(1)}, f32[512,1024]{1,0:T(8,128)}, u32[]{:S(2)}) copy-start(f32[512,1024]{1,0:T(8,128)} %copy-done.8) | copy-start | bytes 6291460
  299.0 9.4 %copy-start.14 = (bf16[512,512]{1,0:T(8,128)(2,1)S(1)}, bf16[512,512]{1,0:T(8,128)(2,1)}, u32[]{:S(2)}) copy-start(bf16[512,512]{1,0:T(8,128)(2,1)} %param.27) | copy-start | bytes 1572868
  299.0 11.1 %copy-start.27 = (bf16[512,512]{1,0:T(8,128)(2,1)S(1)}, bf16[512,512]{1,0:T(8,128)(2,1)}, u32[]{:S(2)}) copy-start(bf16[512,512]{1,0:T(8,128)(2,1)} %copy-done.26) | copy-start | bytes 1572868
  300.7 10.3 %collective-permute-start.7 = (bf16[32,512]{1,0:T(8,128)(2,1)S(1)}, bf16[32,512]{1,0:T(8,128)(2,1)S(1)}, u32[]{:S(2)}, u32[]{:S(2)}) collective-permute-start(bf16[32,512]{1,0:T(8,128)(2,1)S(1)} %get-tuple-element.28), channel_id=1, source_target_pairs={{0,1},{1,2},{2,3},{3,4},{4,5},{5,6},{6,7},{8,9},{9,10},{10,11},{11... | collective-permute-start | bytes 98312 | tf_op jit(solution)/shard_map/ppermute | solution.py:12
  303.9 7.2 %collective-permute-start.6 = (bf16[32,512]{1,0:T(8,128)(2,1)S(1)}, bf16[32,512]{1,0:T(8,128)(2,1)S(1)}, u32[]{:S(2)}, u32[]{:S(2)}) collective-permute-start(bf16[32,512]{1,0:T(8,128)(2,1)S(1)} %get-tuple-element.29), channel_id=1, source_target_pairs={{1,0},{2,1},{3,2},{4,3},{5,4},{6,5},{7,6},{9,8},{10,9},{11,10},{12... | collective-permute-start | bytes 98312 | tf_op jit(solution)/shard_map/ppermute | solution.py:12
  305.2 5.9 %collective-permute-start.5 = (bf16[32,512]{1,0:T(8,128)(2,1)S(1)}, bf16[32,512]{1,0:T(8,128)(2,1)S(1)}, u32[]{:S(2)}, u32[]{:S(2)}) collective-permute-start(bf16[32,512]{1,0:T(8,128)(2,1)S(1)} %get-tuple-element.30), channel_id=1, source_target_pairs={{0,8},{8,16},{16,24},{1,9},{9,17},{17,25},{2,10},{10,18},{18,26},{... | collective-permute-start | bytes 98312 | tf_op jit(solution)/shard_map/ppermute | solution.py:12
  307.1 6.4 %collective-permute-start.4 = (bf16[32,512]{1,0:T(8,128)(2,1)S(1)}, bf16[32,512]{1,0:T(8,128)(2,1)S(1)}, u32[]{:S(2)}, u32[]{:S(2)}) collective-permute-start(bf16[32,512]{1,0:T(8,128)(2,1)S(1)} %get-tuple-element.27), channel_id=1, source_target_pairs={{8,0},{16,8},{24,16},{9,1},{17,9},{25,17},{10,2},{18,10},{26,18},{... | collective-permute-start | bytes 98312 | tf_op jit(solution)/shard_map/ppermute | solution.py:12
  315.2 138.9 %copy-start.18 = (f32[512,512]{1,0:T(8,128)}, f32[512,512]{1,0:T(8,128)S(1)}, u32[]{:S(2)}) copy-start(f32[512,512]{1,0:T(8,128)S(1)} %scatter_custom_fusion.5) | copy-start | bytes 3145732
  446.7 4.8 %copy-start.17 = (f32[512,512]{1,0:T(8,128)S(1)}, f32[512,512]{1,0:T(8,128)}, u32[]{:S(2)}) copy-start(f32[512,512]{1,0:T(8,128)} %get-tuple-element.13) | copy-start | bytes 3145732
  446.7 5.9 %copy-start.13 = (f32[1024,512]{1,0:T(8,128)S(1)}, f32[1024,512]{1,0:T(8,128)}, u32[]{:S(2)}) copy-start(f32[1024,512]{1,0:T(8,128)} %get-tuple-element.14) | copy-start | bytes 6291460
  449.1 5.0 %copy-start.16 = (f32[512,512]{1,0:T(8,128)S(1)}, f32[512,512]{1,0:T(8,128)}, u32[]{:S(2)}) copy-start(f32[512,512]{1,0:T(8,128)} %get-tuple-element.15) | copy-start | bytes 3145732
  451.5 3.7 copy-start.15
  452.5 3.7 copy-start.1
Sparse Core Ops, SparseCore 0:
  256.4 190.1 all-reduce.2
where the time goes:
time: 465 us; the launch traced here: 463 us
  waiting for transfers between devices  241 us (52%)
  other arithmetic  70.5 us (15%)
  local copies, waits for them, and re-layouts  62 us (13%)
  matrix products  37.9 us (8%)
  starting transfers between devices  37.4 us (8%)
  between operations  14.8 us (3%)
    psum x1, waiting for transfers between devices, local(): lax.psum((source_gradient, target_gradient, edge_gradient, inner_gradient...  131 us
    all_to_all x4, waiting for transfers between devices, trade_slots(): lax.all_to_all(buffer, ('row', 'col'), split_axis=0, concat_axis=0, tiled...  107 us
    all_to_all x4, starting transfers between devices, trade_slots(): lax.all_to_all(buffer, ('row', 'col'), split_axis=0, concat_axis=0, tiled...  20.9 us
    ppermute x8, starting transfers between devices, passed_along(): lax.ppermute(value, axis, [(source, source + steps) for source in range(i...  16.5 us
    scatter-add x1, other arithmetic, local(): jax.ops.segment_sum(jax.nn.silu(message_linear), edge_target, count_rows)  14.6 us
    dot_general x6, matrix products, left_product(): lax.dot_general(first, second, (((0,), (0,)), ((), ())), preferred_elemen...  13.9 us
    scatter-add x1, other arithmetic, local(): jax.ops.segment_sum(grad_edges, edge_target, count_rows)  13.7 us
    scatter-add x1, other arithmetic, local(): jax.ops.segment_sum(grad_edges, edge_source, extended.shape[0])  13.6 us
  transfers between devices with their start and end apart: 13, of which 6 were waited for; matrix products, arithmetic and copies ran while one was open for 8% of the time, Pallas kernels for 0%

commit v1 on v0

v1 whole, which is shorter than its diff:
```python
import math

import jax
import jax.numpy as jnp
from jax import lax
from jax.sharding import PartitionSpec as P


def passed_along(value, axis, steps):
    count = lax.axis_size(axis)
    initial, last = (max(0, -steps), min(count, count - steps))
    return lax.ppermute(value, axis, [(source, source + steps) for source in range(initial, last)])


def product(first, second):
    return jnp.dot(first, second, preferred_element_type=jnp.float32)


def left_product(first, second):
    return lax.dot_general(
        first, second, (((0,), (0,)), ((), ())), preferred_element_type=jnp.float32
    )


def right_product(first, second):
    return lax.dot_general(
        first, second, (((1,), (1,)), ((), ())), preferred_element_type=jnp.float32
    )


def silu_slope(value):
    sigma = jax.nn.sigmoid(value)
    return sigma * (1.0 + value * (1.0 - sigma))


def one_hot(index, rows):
    return (index[:, None] == jnp.arange(rows, dtype=jnp.int32)[None, :]).astype(jnp.bfloat16)


def low(value):
    return value.astype(jnp.bfloat16)


def trade_halo(blocks, flip):
    moved = []
    for number, offset in enumerate((1, -1)):
        moved.append(passed_along(blocks[number], "row", offset * flip))
    for number, offset in enumerate((1, -1)):
        moved.append(passed_along(blocks[2 + number], "col", offset * flip))
    return moved


def trade_slots(buffer):
    return lax.all_to_all(buffer, ("row", "col"), split_axis=0, concat_axis=0, tiled=True)


def local(
    nodes,
    cotangent,
    edge_source,
    edge_target,
    halo_lists,
    pool_owner,
    pool_table,
    source_weight,
    target_weight,
    edge_weight,
    inner_weight,
    outer_weight,
    coarse_weight,
):
    devices = lax.axis_size("row") * lax.axis_size("col")
    count_rows, width = nodes.shape
    lists = halo_lists[0]
    halo_rows = lists.shape[1]
    table = pool_table[0]
    capacity = table.shape[0] // devices
    coarse_rows = count_rows // 4
    scale = 1.0 / math.sqrt(count_rows * devices)
    all_lists = lists.reshape(-1)
    owner_hot = one_hot(pool_owner, devices)
    positions = jnp.arange(count_rows, dtype=jnp.int32)
    lower = (positions[:, None] > positions[None, :]).astype(jnp.bfloat16)
    rank = jnp.sum(product(lower, owner_hot) * owner_hot, axis=1).astype(jnp.int32)
    slot = pool_owner * capacity + rank
    slot_hot = one_hot(slot, devices * capacity)
    member = (jnp.arange(coarse_rows, dtype=jnp.int32)[:, None] == table[None, :]).astype(
        jnp.bfloat16
    )
    count = jnp.maximum(jnp.sum(member, axis=1, dtype=jnp.float32), 1.0)[:, None]

    def toward_owners(values):
        return product(member, trade_slots(low(left_product(slot_hot, values))))

    def toward_sources(values):
        return product(slot_hot, trade_slots(low(left_product(member, values))))

    list_hot = one_hot(all_lists, count_rows)
    picked = low(product(list_hot, nodes)).reshape(4, halo_rows, width)
    received = trade_halo([picked[number] for number in range(4)], 1)
    pooled_cotangent = toward_owners(cotangent)
    extended = jnp.concatenate([nodes] + received, axis=0)
    source_hot = one_hot(edge_source, extended.shape[0])
    target_hot = one_hot(edge_target, count_rows)
    source_side = low(product(extended, source_weight))
    target_side = low(product(nodes, target_weight))
    edge_linear = product(source_hot, source_side) + product(target_hot, target_side)
    edge_hidden = low(jax.nn.silu(edge_linear))
    message_linear = product(edge_hidden, edge_weight)
    aggregate = low(left_product(target_hot, low(jax.nn.silu(message_linear))))
    joined = jnp.concatenate([nodes, aggregate], axis=1)
    node_linear = product(joined, inner_weight)
    node_hidden = low(jax.nn.silu(node_linear))
    refined = low(nodes.astype(jnp.float32) + product(node_hidden, outer_weight))
    coarse = low(toward_owners(refined) / count)
    coarse_linear = product(coarse, coarse_weight)
    coarse_update = low(jax.nn.silu(coarse_linear))
    grad_coarse = low(pooled_cotangent * silu_slope(coarse_linear))
    coarse_share = low(right_product(grad_coarse, coarse_weight) / count)
    share_rows = toward_sources(coarse_share)
    updated = low(refined.astype(jnp.float32) + toward_sources(coarse_update))
    coarse_gradient = left_product(coarse, grad_coarse)
    grad_refined = cotangent.astype(jnp.float32) + share_rows
    refined_low = low(grad_refined)
    outer_gradient = left_product(node_hidden, refined_low)
    grad_hidden = low(right_product(refined_low, outer_weight) * silu_slope(node_linear))
    inner_gradient = left_product(joined, grad_hidden)
    grad_joined = right_product(grad_hidden, inner_weight)
    grad_aggregate = low(grad_joined[:, width:])
    grad_message = low(product(target_hot, grad_aggregate) * silu_slope(message_linear))
    edge_gradient = left_product(edge_hidden, grad_message)
    grad_edges = low(right_product(grad_message, edge_weight) * silu_slope(edge_linear))
    grad_sources = low(left_product(source_hot, grad_edges))
    grad_targets = low(left_product(target_hot, grad_edges))
    source_gradient = left_product(extended, grad_sources)
    target_gradient = left_product(nodes, grad_targets)
    gradients = (
        source_gradient,
        target_gradient,
        edge_gradient,
        inner_gradient,
        outer_gradient,
        coarse_gradient,
    )
    sizes = [gradient.shape[0] for gradient in gradients]
    stacked = jnp.concatenate([low(gradient * scale) for gradient in gradients], axis=0)
    share = lax.psum_scatter(stacked, ("row", "col"), scatter_dimension=0, tiled=True)
    summed = lax.all_gather(share, ("row", "col"), axis=0, tiled=True).astype(jnp.float32)
    starts = [sum(sizes[:number]) for number in range(len(sizes))]
    totals = [
        lax.slice_in_dim(summed, start, start + size, axis=0)
        for start, size in zip(starts, sizes)
    ]
    grad_extended = right_product(grad_sources, source_weight)
    back_blocks = low(grad_extended[count_rows:]).reshape(4, halo_rows, width)
    returned = trade_halo([back_blocks[number] for number in range(4)], -1)
    node_gradient = (
        grad_refined
        + grad_joined[:, :width]
        + right_product(grad_targets, target_weight)
        + grad_extended[:count_rows]
        + left_product(list_hot, jnp.concatenate(returned, axis=0))
    )
    return (updated, node_gradient, *totals)


def solution(mesh):
    in_specs = (
        P(("row", "col"), None),
        P(("row", "col"), None),
        P(("row", "col")),
        P(("row", "col")),
        P(("row", "col"), None, None),
        P(("row", "col")),
        P(("row", "col"), None),
        P(),
        P(),
        P(),
        P(),
        P(),
        P(),
    )
    out_specs = (P(("row", "col"), None), P(("row", "col"), None), P(), P(), P(), P(), P(), P())
    return jax.shard_map(local, mesh=mesh, in_specs=in_specs, out_specs=out_specs, check_vma=False)
```

time: 465 us -> 385 us (0.83)
  other arithmetic: 70.5 us -> 0.83 us
  local copies, waits for them, and re-layouts: 62 us -> 14.1 us
  blocking collectives: 0 us -> 29.7 us
  matrix products: 37.9 us -> 63.4 us
  waiting for transfers between devices: 241 us -> 228 us
    reduce_scatter x0 -> x1, waiting for transfers between devices: none -> 138 us  [local(): lax.psum_scatter(stacked, ('row', 'col'), scatter_dimension=0, tiled=True)]
    psum x1 -> x0, waiting for transfers between devices: 131 us -> none  [local(): lax.psum((source_gradient, target_gradient, edge_gradient, inner_gradient...]
    gather x11 -> x0, local copies, waits for them, and re-layouts: 47.7 us -> none  [the longest x1 9.21 us: local(): jnp.take(grad_aggregate, edge_target, axis=0) * silu_slope(message_linear)]
    scatter-add x4 -> x0, other arithmetic: 43.6 us -> none  [the longest x1 14.6 us: local(): jax.ops.segment_sum(jax.nn.silu(message_linear), edge_target, count_rows)]
    all_to_all x4 -> x3, waiting for transfers between devices: 107 us -> 67.7 us  [trade_slots(): lax.all_to_all(buffer, ('row', 'col'), split_axis=0, concat_axis=0, tiled...]
    all_to_all x0 -> x1, blocking collectives: none -> 29.7 us  [trade_slots(): lax.all_to_all(buffer, ('row', 'col'), split_axis=0, concat_axis=0, tiled...]
    all_gather x0 -> x1, waiting for transfers between devices: none -> 22.4 us  [local(): lax.all_gather(share, ('row', 'col'), axis=0, tiled=True)]
    dot_general x9 -> x13, matrix products: 11.9 us -> 28.8 us  [product(): return jnp.dot(first, second, preferred_element_type=jnp.float32)]
  transfers between devices with their start and end apart: 13 -> 13, of which waited for: 6 -> 5; matrix products, arithmetic and copies ran while one was open for 8% -> 4% of each run, Pallas kernels for 0% -> 0%
where the time goes in v1:
time: 385 us; the launch traced here: 384 us
  waiting for transfers between devices  228 us (59%)
  matrix products  63.4 us (16%)
  starting transfers between devices  32.8 us (9%)
  blocking collectives  29.7 us (8%)
  between operations  14.8 us (4%)
  local copies, waits for them, and re-layouts  14.1 us (4%)
    reduce_scatter x1, waiting for transfers between devices, local(): lax.psum_scatter(stacked, ('row', 'col'), scatter_dimension=0, tiled=True)  138 us
    all_to_all x3, waiting for transfers between devices, trade_slots(): lax.all_to_all(buffer, ('row', 'col'), split_axis=0, concat_axis=0, tiled...  67.7 us
    all_to_all x1, blocking collectives, trade_slots(): lax.all_to_all(buffer, ('row', 'col'), split_axis=0, concat_axis=0, tiled...  29.7 us
    dot_general x13, matrix products, product(): return jnp.dot(first, second, preferred_element_type=jnp.float32)  28.8 us
    dot_general x14, matrix products, left_product(): lax.dot_general(first, second, (((0,), (0,)), ((), ())), preferred_elemen...  27.4 us
    all_gather x1, waiting for transfers between devices, local(): lax.all_gather(share, ('row', 'col'), axis=0, tiled=True)  22.4 us
    ppermute x8, starting transfers between devices, passed_along(): lax.ppermute(value, axis, [(source, source + steps) for source in range(i...  20 us
    all_to_all x3, starting transfers between devices, trade_slots(): lax.all_to_all(buffer, ('row', 'col'), split_axis=0, concat_axis=0, tiled...  12.5 us
  transfers between devices with their start and end apart: 13, of which 5 were waited for; matrix products, arithmetic and copies ran while one was open for 4% of the time, Pallas kernels for 0%

profile of v1, /device:TPU:0, one launch (start us, length us, event | category | flops | bytes accessed | tf_op | source)
XLA Modules:
  0.0 383.8 jit_solution(4225558319143161843)
XLA Ops:
  7.2 0.9 eq.88
  8.0 1.3 convolution_convert_fusion.4
  9.4 1.3 collective-permute-start.3
  10.7 3.0 collective-permute-start.2
  13.7 1.3 collective-permute-start.1
  15.0 5.6 %collective-permute-start = (bf16[32,512]{1,0:T(8,128)(2,1)S(1)}, bf16[32,512]{1,0:T(8,128)(2,1)S(1)}, u32[]{:S(2)}, u32[]{:S(2)}) collective-permute-start(bf16[32,512]{1,0:T(8,128)(2,1)S(1)} %get-tuple-element.20), channel_id=1, source_target_pairs={{0,8},{8,16},{16,24},{1,9},{9,17},{17,25},{2,10},{10,18},{18,26},{... | collective-permute-start | bytes 98312 | tf_op jit(solution)/shard_map/ppermute | solution.py:12
  20.6 1.0 fusion.42
  21.6 0.7 convert_add_fusion
  22.3 1.1 constant_dynamic-update-slice_fusion.4
  23.4 1.3 copy.24
  24.8 5.5 %fusion.1 = f32[2048,512]{1,0:T(8,128)} fusion(s32[2048]{0:T(1024)} %param.15, bf16[640,512]{1,0:T(8,128)(2,1)S(1)} %constant_dynamic-update-slice_fusion, bf16[512,512]{1,0:T(8,128)(2,1)} %param.20), kind=kOutput, calls=%fused_computation.2 | convolution fusion | flops 1679360000 | bytes 5382144 | tf_op jit(solution)/shard_map/dot_general | solution.py:16
  30.4 5.8 %fusion.6 = f32[2048,512]{1,0:T(8,128)} fusion(f32[2048,512]{1,0:T(8,128)} %fusion.1, s32[2048]{0:T(1024)S(1)} %copy-done.22, bf16[512,512]{1,0:T(8,128)(2,1)S(1)} %copy-done.2, bf16[512,512]{1,0:T(8,128)(2,1)S(1)} %copy-done.7), kind=kOutput, calls=%fused_computation.14 | convolution fusion | flops 1344536576 | bytes 9445376 | tf_op jit(solution)/shard_map/dot_general | solution.py:16
  36.2 3.6 fusion.73
  39.8 2.2 fusion.26
  42.0 0.7 fusion.47
  42.7 0.5 copy-done.26
  43.2 0.5 fusion.30
  43.7 1.8 fusion.17
  45.5 5.4 %all-to-all-start = ((bf16[32,32,512]{2,1,0:T(8,128)(2,1)}), bf16[32,32,512]{2,1,0:T(8,128)(2,1)S(1)}, u32[]{:S(2)}, u32[]{:S(2)}) async-start(bf16[32,32,512]{2,1,0:T(8,128)(2,1)} %bitcast.51), calls=%async_computation | async-start | bytes 2097152 | tf_op jit(solution)/shard_map/all_to_all | solution.py:54
  50.9 2.9 fusion.18
  53.8 23.3 %all-to-all-done = bf16[32,32,512]{2,1,0:T(8,128)(2,1)S(1)} async-done(((bf16[32,32,512]{2,1,0:T(8,128)(2,1)}), bf16[32,32,512]{2,1,0:T(8,128)(2,1)S(1)}, u32[]{:S(2)}, u32[]{:S(2)}) %all-to-all-start) | async-done | bytes 1048608 | tf_op jit(solution)/shard_map/all_to_all | solution.py:54
  77.1 3.7 all-to-all-start.2
  80.9 0.0 reduce-scatter.2.cloned.1.call-start
  80.9 0.1 convert_reduce_fusion
  81.1 0.5 copy-done.30
  81.6 0.3 fusion.40
  81.9 0.2 fusion.78
  82.2 24.9 %all-to-all-done.2 = bf16[32,32,512]{2,1,0:T(8,128)(2,1)} async-done(((bf16[32,32,512]{2,1,0:T(8,128)(2,1)}), bf16[32,32,512]{2,1,0:T(8,128)(2,1)}, u32[]{:S(2)}, u32[]{:S(2)}) %all-to-all-start.2) | async-done | bytes 1048608 | tf_op jit(solution)/shard_map/all_to_all | solution.py:54
  107.1 2.2 fusion.41
  109.3 1.6 convolution_convert_fusion
  110.9 29.7 %all_to_all.48 = bf16[32,32,512]{2,1,0:T(8,128)(2,1)S(1)} all-to-all(bf16[32,32,512]{2,1,0:T(8,128)(2,1)S(1)} %bitcast.52), channel_id=1, replica_groups=mesh['row'=4,'col'=8] {'row','col'}, dimensions={0} | all-to-all | bytes 2097152 | tf_op jit(solution)/shard_map/all_to_all | solution.py:54
  140.6 1.8 fusion.21
  142.5 0.6 fusion.31
  143.1 0.8 copy-done.14
  143.9 0.7 fusion.79
  144.7 1.3 copy-done.3
  146.0 2.8 multiply_convert_fusion.1
  148.9 2.4 multiply_convert_fusion
  151.3 1.7 fusion.27
  153.0 2.0 fusion.23
  155.0 1.3 fusion.38
  156.2 1.3 copy.26
  157.5 2.6 fusion.29
  160.1 0.8 constant_dynamic-update-slice_fusion.5
  161.0 4.4 %fusion.34 = bf16[3584,512]{1,0:T(8,128)(2,1)} fusion(bf16[3584,512]{1,0:T(8,128)(2,1)} %constant_dynamic-update-slice_fusion.5, bf16[2048,512]{1,0:T(8,128)(2,1)S(1)} %copy-done.41, f32[2048,512]{1,0:T(8,128)} %fusion.6), kind=kOutput, calls=%fused_computation.57 | convolution fusion | flops 1079508992 | bytes 6815744 | tf_op jit(solution)/shard_map/dot_general | solution.py:20
  165.4 1.7 fusion.19
  167.2 1.3 fusion.36
  168.5 1.1 fusion.25
  169.6 0.3 all-gather.2.cloned.1.call-start
  169.9 138.2 %reduce-scatter.2.cloned.1.call-done = bf16[112,512]{1,0:T(8,128)(2,1)} async-done(((bf16[3584,512]{1,0:T(8,128)(2,1)}), bf16[112,512]{1,0:T(8,128)(2,1)}) %reduce-scatter.2.cloned.1.call-update) | async-done | bytes 114704 | tf_op jit(solution)/shard_map/reduce_scatter | solution.py:147
  308.1 1.5 convolution_convert_fusion.1
  309.6 3.4 all-to-all-start.1
  313.0 1.9 fusion.77
  315.0 1.3 collective-permute-start.4
  316.3 1.9 collective-permute-start.7
  318.2 1.3 collective-permute-start.6
  319.5 4.3 %collective-permute-start.5 = (bf16[32,512]{1,0:T(8,128)(2,1)S(1)}, bf16[32,512]{1,0:T(8,128)(2,1)S(1)}, u32[]{:S(2)}, u32[]{:S(2)}) collective-permute-start(bf16[32,512]{1,0:T(8,128)(2,1)S(1)} %get-tuple-element.16), channel_id=1, source_target_pairs={{0,8},{8,16},{16,24},{1,9},{9,17},{17,25},{2,10},{10,18},{18,26},{... | collective-permute-start | bytes 98312 | tf_op jit(solution)/shard_map/ppermute | solution.py:12
  323.8 1.5 fusion.22
  325.3 19.5 %all-to-all-done.1 = bf16[32,32,512]{2,1,0:T(8,128)(2,1)} async-done(((bf16[32,32,512]{2,1,0:T(8,128)(2,1)}), bf16[32,32,512]{2,1,0:T(8,128)(2,1)}, u32[]{:S(2)}, u32[]{:S(2)}) %all-to-all-start.1) | async-done | bytes 1048608 | tf_op jit(solution)/shard_map/all_to_all | solution.py:54
  344.8 2.9 fusion.37
  347.8 1.4 convolution_add_fusion
  349.2 22.4 %all-gather.2.cloned.1.call-done = bf16[3584,512]{1,0:T(8,128)(2,1)} async-done(((bf16[112,512]{1,0:T(8,128)(2,1)}), bf16[3584,512]{1,0:T(8,128)(2,1)}) %all-gather.2.cloned.1.call-update) | async-done | bytes 3670032 | tf_op jit(solution)/shard_map/all_gather | solution.py:148
  371.5 3.0 slice.97
  374.5 2.5 fusion.74
  (97 shorter events, 0.3 us)
Async XLA Ops:
  7.2 34.8 %copy-start = (bf16[1024,512]{1,0:T(8,128)(2,1)S(1)}, bf16[1024,512]{1,0:T(8,128)(2,1)}, u32[]{:S(2)}) copy-start(bf16[1024,512]{1,0:T(8,128)(2,1)} %param.23) | copy-start | bytes 3145732
  9.4 15.4 %collective-permute-start.3 = (bf16[32,512]{1,0:T(8,128)(2,1)S(1)}, bf16[32,512]{1,0:T(8,128)(2,1)S(1)}, u32[]{:S(2)}, u32[]{:S(2)}) collective-permute-start(bf16[32,512]{1,0:T(8,128)(2,1)S(1)} %get-tuple-element.17), channel_id=1, source_target_pairs={{1,0},{2,1},{3,2},{4,3},{5,4},{6,5},{7,6},{9,8},{10,9},{11,10},{12... | collective-permute-start | bytes 98312 | tf_op jit(solution)/shard_map/ppermute | solution.py:12
  10.7 14.0 %collective-permute-start.2 = (bf16[32,512]{1,0:T(8,128)(2,1)S(1)}, bf16[32,512]{1,0:T(8,128)(2,1)S(1)}, u32[]{:S(2)}, u32[]{:S(2)}) collective-permute-start(bf16[32,512]{1,0:T(8,128)(2,1)S(1)} %get-tuple-element.18), channel_id=1, source_target_pairs={{0,1},{1,2},{2,3},{3,4},{4,5},{5,6},{6,7},{8,9},{9,10},{10,11},{11... | collective-permute-start | bytes 98312 | tf_op jit(solution)/shard_map/ppermute | solution.py:12
  13.7 11.0 %collective-permute-start.1 = (bf16[32,512]{1,0:T(8,128)(2,1)S(1)}, bf16[32,512]{1,0:T(8,128)(2,1)S(1)}, u32[]{:S(2)}, u32[]{:S(2)}) collective-permute-start(bf16[32,512]{1,0:T(8,128)(2,1)S(1)} %get-tuple-element.19), channel_id=1, source_target_pairs={{8,0},{16,8},{24,16},{9,1},{17,9},{25,17},{10,2},{18,10},{26,18},{... | collective-permute-start | bytes 98312 | tf_op jit(solution)/shard_map/ppermute | solution.py:12
  15.0 9.6 %collective-permute-start = (bf16[32,512]{1,0:T(8,128)(2,1)S(1)}, bf16[32,512]{1,0:T(8,128)(2,1)S(1)}, u32[]{:S(2)}, u32[]{:S(2)}) collective-permute-start(bf16[32,512]{1,0:T(8,128)(2,1)S(1)} %get-tuple-element.20), channel_id=1, source_target_pairs={{0,8},{8,16},{16,24},{1,9},{9,17},{17,25},{2,10},{10,18},{18,26},{... | collective-permute-start | bytes 98312 | tf_op jit(solution)/shard_map/ppermute | solution.py:12
  22.3 28.6 %copy-start.24 = (s32[512]{0:T(512)}, s32[512]{0:T(512)S(1)}, u32[]{:S(2)}) copy-start(s32[512]{0:T(512)S(1)} %convert_add_fusion) | copy-start | bytes 6148
  24.6 17.3 %copy-start.17 = (bf16[512,512]{0,1:T(8,128)(2,1)}, bf16[512,512]{0,1:T(8,128)(2,1)S(1)}, u32[]{:S(2)}) copy-start(bf16[512,512]{0,1:T(8,128)(2,1)S(1)} %copy.24) | copy-start | bytes 1572868
  24.7 5.6 %copy-start.19 = (bf16[640,512]{1,0:T(8,128)(2,1)}, bf16[640,512]{1,0:T(8,128)(2,1)S(1)}, u32[]{:S(2)}) copy-start(bf16[640,512]{1,0:T(8,128)(2,1)S(1)} %constant_dynamic-update-slice_fusion) | copy-start | bytes 1966084
  24.8 5.6 %copy-start.2 = (bf16[512,512]{1,0:T(8,128)(2,1)S(1)}, bf16[512,512]{1,0:T(8,128)(2,1)}, u32[]{:S(2)}) copy-start(bf16[512,512]{1,0:T(8,128)(2,1)} %param.13) | copy-start | bytes 1572868
  24.8 5.6 %copy-start.7 = (bf16[512,512]{1,0:T(8,128)(2,1)S(1)}, bf16[512,512]{1,0:T(8,128)(2,1)}, u32[]{:S(2)}) copy-start(bf16[512,512]{1,0:T(8,128)(2,1)} %param.21) | copy-start | bytes 1572868
  24.8 5.6 %copy-start.22 = (s32[2048]{0:T(1024)S(1)}, s32[2048]{0:T(1024)}, u32[]{:S(2)}) copy-start(s32[2048]{0:T(1024)} %param.16) | copy-start | bytes 24580
  39.8 2.2 copy-start.38
  42.0 1.7 copy-start.36
  42.0 1.2 copy-start.26
  43.2 2.3 copy-start.33
  43.7 1.8 copy-start.32
  45.5 35.4 %copy-start.23 = (s32[1,1024]{1,0:T(1,128)S(1)}, s32[1,1024]{1,0:T(1,128)}, u32[]{:S(2)}) copy-start(s32[1,1024]{1,0:T(1,128)} %param.19) | copy-start | bytes 12292
  45.5 31.6 %all-to-all-start = ((bf16[32,32,512]{2,1,0:T(8,128)(2,1)}), bf16[32,32,512]{2,1,0:T(8,128)(2,1)S(1)}, u32[]{:S(2)}, u32[]{:S(2)}) async-start(bf16[32,32,512]{2,1,0:T(8,128)(2,1)} %bitcast.51), calls=%async_computation | async-start | bytes 2097152 | tf_op jit(solution)/shard_map/all_to_all | solution.py:54
  50.9 31.0 %copy-start.16 = (bf16[512,512]{1,0:T(8,128)(2,1)S(1)}, bf16[512,512]{1,0:T(8,128)(2,1)}, u32[]{:S(2)}) copy-start(bf16[512,512]{1,0:T(8,128)(2,1)} %param.25) | copy-start | bytes 1572868
  77.1 30.0 %all-to-all-start.2 = ((bf16[32,32,512]{2,1,0:T(8,128)(2,1)}), bf16[32,32,512]{2,1,0:T(8,128)(2,1)}, u32[]{:S(2)}, u32[]{:S(2)}) async-start(bf16[32,32,512]{2,1,0:T(8,128)(2,1)} %bitcast.50), calls=%async_computation.2 | async-start | bytes 2097152 | tf_op jit(solution)/shard_map/all_to_all | solution.py:54
  80.9 227.2 %reduce-scatter.2.cloned.1.call-start = ((), (), s32[]{:S(2)}) async-start(), calls=%async_computation.5 | async-start | bytes 3784704 | tf_op jit(solution)/shard_map/reduce_scatter | solution.py:147
  81.1 0.5 copy-start.30
  81.9 60.5 %copy-start.20 = (bf16[128,512]{1,0:T(8,128)(2,1)}, bf16[128,512]{1,0:T(8,128)(2,1)S(1)}, u32[]{:S(2)}) copy-start(bf16[128,512]{1,0:T(8,128)(2,1)S(1)} %fusion.40) | copy-start | bytes 393220
  110.9 31.5 %copy-start.27 = (bf16[512,512]{1,0:T(8,128)(2,1)S(1)}, bf16[512,512]{1,0:T(8,128)(2,1)}, u32[]{:S(2)}) copy-start(bf16[512,512]{1,0:T(8,128)(2,1)} %param.24) | copy-start | bytes 1572868
  110.9 31.5 %copy-start.34 = (f32[512,512]{1,0:T(8,128)S(1)}, f32[512,512]{1,0:T(8,128)}, u32[]{:S(2)}) copy-start(f32[512,512]{1,0:T(8,128)} %copy-done.33) | copy-start | bytes 3145732
  142.5 24.7 %copy-start.9 = (f32[512,512]{1,0:T(8,128)}, f32[512,512]{1,0:T(8,128)S(1)}, u32[]{:S(2)}) copy-start(f32[512,512]{1,0:T(8,128)S(1)} %fusion.21) | copy-start | bytes 3145732
  142.5 3.5 copy-start.39
  143.1 0.8 copy-start.14
  144.7 1.3 copy-start.3
  146.0 2.9 copy-start.6
  146.0 2.9 copy-start.28
  148.9 2.4 copy-start.40
  151.3 1.7 copy-start.29
  153.0 2.0 copy-start.12
  155.0 10.4 %copy-start.11 = (bf16[640,512]{1,0:T(8,128)(2,1)}, bf16[640,512]{1,0:T(8,128)(2,1)S(1)}, u32[]{:S(2)}) copy-start(bf16[640,512]{1,0:T(8,128)(2,1)S(1)} %fusion.23) | copy-start | bytes 1966084
  157.5 3.5 copy-start.41
  161.0 4.4 %copy-start.15 = (bf16[512,512]{1,0:T(8,128)(2,1)S(1)}, bf16[512,512]{1,0:T(8,128)(2,1)}, u32[]{:S(2)}) copy-start(bf16[512,512]{1,0:T(8,128)(2,1)} %copy-done.14) | copy-start | bytes 1572868
  161.0 4.4 %copy-start.18 = (bf16[512,512]{0,1:T(8,128)(2,1)S(1)}, bf16[512,512]{0,1:T(8,128)(2,1)}, u32[]{:S(2)}) copy-start(bf16[512,512]{0,1:T(8,128)(2,1)} %copy-done.17) | copy-start | bytes 1572868
  161.0 4.4 %copy-start.37 = (bf16[512,512]{0,1:T(8,128)(2,1)S(1)}, bf16[512,512]{0,1:T(8,128)(2,1)}, u32[]{:S(2)}) copy-start(bf16[512,512]{0,1:T(8,128)(2,1)} %copy-done.36) | copy-start | bytes 1572868
  165.4 1.7 copy-start.35
  167.1 1.3 copy-start.21
  167.2 1.3 copy-start.31
  169.6 154.2 %copy-start.4 = (f32[512,1024]{1,0:T(8,128)S(1)}, f32[512,1024]{1,0:T(8,128)}, u32[]{:S(2)}) copy-start(f32[512,1024]{1,0:T(8,128)} %copy-done.3) | copy-start | bytes 6291460
  169.6 201.9 %all-gather.2.cloned.1.call-start = ((), (), s32[]{:S(2)}) async-start(), calls=%async_computation.6 | async-start | bytes 3784704 | tf_op jit(solution)/shard_map/all_gather | solution.py:148
  309.6 35.2 %all-to-all-start.1 = ((bf16[32,32,512]{2,1,0:T(8,128)(2,1)}), bf16[32,32,512]{2,1,0:T(8,128)(2,1)}, u32[]{:S(2)}, u32[]{:S(2)}) async-start(bf16[32,32,512]{2,1,0:T(8,128)(2,1)} %bitcast.48), calls=%async_computation.1 | async-start | bytes 2097152 | tf_op jit(solution)/shard_map/all_to_all | solution.py:54
  313.0 10.8 %copy-start.8 = (bf16[512,512]{1,0:T(8,128)(2,1)S(1)}, bf16[512,512]{1,0:T(8,128)(2,1)}, u32[]{:S(2)}) copy-start(bf16[512,512]{1,0:T(8,128)(2,1)} %param.21) | copy-start | bytes 1572868
  313.0 10.8 %copy-start.10 = (f32[512,512]{1,0:T(8,128)S(1)}, f32[512,512]{1,0:T(8,128)}, u32[]{:S(2)}) copy-start(f32[512,512]{1,0:T(8,128)} %copy-done.9) | copy-start | bytes 3145732
  313.0 10.8 %copy-start.13 = (bf16[512,512]{1,0:T(8,128)(2,1)S(1)}, bf16[512,512]{1,0:T(8,128)(2,1)}, u32[]{:S(2)}) copy-start(bf16[512,512]{1,0:T(8,128)(2,1)} %copy-done.12) | copy-start | bytes 1572868
  313.0 31.8 %copy-start.25 = (s32[512]{0:T(512)S(1)}, s32[512]{0:T(512)}, u32[]{:S(2)}) copy-start(s32[512]{0:T(512)} %copy-done.24) | copy-start | bytes 6148
  315.0 32.8 %collective-permute-start.4 = (bf16[32,512]{1,0:T(8,128)(2,1)S(1)}, bf16[32,512]{1,0:T(8,128)(2,1)S(1)}, u32[]{:S(2)}, u32[]{:S(2)}) collective-permute-start(bf16[32,512]{1,0:T(8,128)(2,1)S(1)} %get-tuple-element.13), channel_id=1, source_target_pairs={{8,0},{16,8},{24,16},{9,1},{17,9},{25,17},{10,2},{18,10},{26,18},{... | collective-permute-start | bytes 98312 | tf_op jit(solution)/shard_map/ppermute | solution.py:12
  316.3 31.5 %collective-permute-start.7 = (bf16[32,512]{1,0:T(8,128)(2,1)S(1)}, bf16[32,512]{1,0:T(8,128)(2,1)S(1)}, u32[]{:S(2)}, u32[]{:S(2)}) collective-permute-start(bf16[32,512]{1,0:T(8,128)(2,1)S(1)} %get-tuple-element.14), channel_id=1, source_target_pairs={{0,1},{1,2},{2,3},{3,4},{4,5},{5,6},{6,7},{8,9},{9,10},{10,11},{11... | collective-permute-start | bytes 98312 | tf_op jit(solution)/shard_map/ppermute | solution.py:12
  318.2 29.5 %collective-permute-start.6 = (bf16[32,512]{1,0:T(8,128)(2,1)S(1)}, bf16[32,512]{1,0:T(8,128)(2,1)S(1)}, u32[]{:S(2)}, u32[]{:S(2)}) collective-permute-start(bf16[32,512]{1,0:T(8,128)(2,1)S(1)} %get-tuple-element.15), channel_id=1, source_target_pairs={{1,0},{2,1},{3,2},{4,3},{5,4},{6,5},{7,6},{9,8},{10,9},{11,10},{12... | collective-permute-start | bytes 98312 | tf_op jit(solution)/shard_map/ppermute | solution.py:12
  319.5 28.2 %collective-permute-start.5 = (bf16[32,512]{1,0:T(8,128)(2,1)S(1)}, bf16[32,512]{1,0:T(8,128)(2,1)S(1)}, u32[]{:S(2)}, u32[]{:S(2)}) collective-permute-start(bf16[32,512]{1,0:T(8,128)(2,1)S(1)} %get-tuple-element.16), channel_id=1, source_target_pairs={{0,8},{8,16},{16,24},{1,9},{9,17},{17,25},{2,10},{10,18},{18,26},{... | collective-permute-start | bytes 98312 | tf_op jit(solution)/shard_map/ppermute | solution.py:12
  325.3 22.4 %copy-start.5 = (f32[512,512]{1,0:T(8,128)S(1)}, f32[512,512]{1,0:T(8,128)}, u32[]{:S(2)}) copy-start(f32[512,512]{1,0:T(8,128)} %fusion.22) | copy-start | bytes 3145732
  371.5 3.0 copy-start.1
Sparse Core Ops, SparseCore 0:
  169.7 138.3 reduce-scatter.1
  311.4 60.1 all-gather.1

commit v2 on v1

--- a/solution.py
+++ b/solution.py
@@ -1,8 +1,11 @@
+import functools
 import math
 
 import jax
 import jax.numpy as jnp
 from jax import lax
+from jax.experimental import pallas as pl
+from jax.experimental.pallas import tpu as pltpu
 from jax.sharding import PartitionSpec as P
 
 
@@ -52,6 +55,192 @@
 
 def trade_slots(buffer):
     return lax.all_to_all(buffer, ("row", "col"), split_axis=0, concat_axis=0, tiled=True)
+
+
+class Summation:
+    def __init__(self, rows, cols, own, land, out, send, recv):
+        self.rows, self.cols, self.devices = rows, cols, rows * cols
+        self.bits = cols.bit_length() - 1
+        self.own, self.land, self.out, self.send, self.recv = own, land, out, send, recv
+        self.row, self.col = lax.axis_index("row"), lax.axis_index("col")
+        self.orders = []
+        rest = list(range(1, self.bits))
+        for half in range(2):
+            self.orders.append([0] + (rest if half == 0 else rest[::-1]))
+        self.bases = []
+        for order in self.orders:
+            base, bases = jnp.int32(0), [jnp.int32(0)]
+            for stage, bit in enumerate(order):
+                base = base + self.digit(bit) * (self.devices >> (stage + 1))
+                bases.append(base)
+            self.bases.append(bases)
+        self.steps = 2 * (self.bits + 1)
+
+    @staticmethod
+    def semaphores(rows, cols):
+        return 2 * (cols.bit_length() - 1 + rows - 1)
+
+    def digit(self, bit):
+        return lax.rem(lax.div(self.col, jnp.int32(1 << bit)), jnp.int32(2))
+
+    def across(self, bit):
+        return self.col + (1 - 2 * self.digit(bit)) * (1 << bit)
+
+    def along(self, step):
+        return lax.rem(self.row + step, jnp.int32(self.rows))
+
+    def copy(self, half, number, source, target, row, col):
+        return pltpu.make_async_remote_copy(
+            src_ref=source,
+            dst_ref=target,
+            send_sem=self.send.at[half, number],
+            recv_sem=self.recv.at[half, number],
+            device_id=(row, col),
+            device_id_type=pl.DeviceIdType.MESH,
+        )
+
+    def copies(self, half, step):
+        bits, bases = self.bits, self.bases[half]
+        found = []
+        if step < bits:
+            size = self.devices >> (step + 1)
+            bit = self.orders[half][step]
+            start = bases[step] + (1 - self.digit(bit)) * size
+            slot = self.devices - (self.devices >> step)
+            found.append(
+                self.copy(
+                    half,
+                    step,
+                    self.own.at[half, pl.ds(start, size)],
+                    self.land.at[half, pl.ds(slot, size)],
+                    self.row,
+                    self.across(bit),
+                )
+            )
+        elif step == bits:
+            for ahead in range(1, self.rows):
+                peer = self.along(ahead)
+                found.append(
+                    self.copy(
+                        half,
+                        bits + ahead - 1,
+                        self.own.at[half, pl.ds(bases[bits] + peer, 1)],
+                        self.land.at[half, pl.ds(self.devices - self.rows + ahead - 1, 1)],
+                        peer,
+                        self.col,
+                    )
+                )
+        elif step == bits + 1:
+            for ahead in range(1, self.rows):
+                mine = self.out.at[half, pl.ds(bases[bits] + self.row, 1)]
+                found.append(
+                    self.copy(
+                        half,
+                        2 * bits + self.rows - 1 + ahead - 1,
+                        mine,
+                        mine,
+                        self.along(ahead),
+                        self.col,
+                    )
+                )
+        else:
+            stage = 2 * bits + 1 - step
+            size = self.devices >> (stage + 1)
+            mine = self.out.at[half, pl.ds(bases[stage + 1], size)]
+            found.append(
+                self.copy(
+                    half,
+                    bits + self.rows - 1 + stage,
+                    mine,
+                    mine,
+                    self.row,
+                    self.across(self.orders[half][stage]),
+                )
+            )
+        return found
+
+    def start(self, half, step):
+        for copy in self.copies(half, step):
+            copy.start()
+
+    def finish(self, half, step):
+        for copy in self.copies(half, step):
+            copy.wait()
+        bits, bases = self.bits, self.bases[half]
+        if step < bits:
+            size = self.devices >> (step + 1)
+            slot = self.devices - (self.devices >> step)
+
+            def add(index, carry):
+                here = bases[step + 1] + index
+                self.own[half, here] = self.own[half, here] + self.land[half, slot + index]
+                return carry
+
+            lax.fori_loop(0, size, add, 0)
+        elif step == bits:
+            total = self.own[half, bases[bits] + self.row].astype(jnp.float32)
+            for ahead in range(1, self.rows):
+                total += self.land[half, self.devices - self.rows + ahead - 1].astype(jnp.float32)
+            self.out[half, bases[bits] + self.row] = total.astype(jnp.bfloat16)
+
+    def begin(self):
+        for half in range(2):
+            self.start(half, 0)
+
+    def advance(self, step):
+        for half in range(2):
+            self.finish(half, step)
+            if step + 1 < self.steps:
+                self.start(half, step + 1)
+
+    def greet(self):
+        barrier = pltpu.get_barrier_semaphore()
+        peers = [(self.row, self.across(bit)) for bit in range(self.bits)]
+        peers += [(self.along(ahead), self.col) for ahead in range(1, self.rows)]
+        for peer in peers:
+            pl.semaphore_signal(
+                barrier, inc=1, device_id=peer, device_id_type=pl.DeviceIdType.MESH
+            )
+        pl.semaphore_wait(barrier, len(peers))
+
+
+def summation_kernel(rows, cols, terms, out, own, land, send, recv, local_sem):
+    summation = Summation(rows, cols, own, land, out, send, recv)
+    load = pltpu.make_async_copy(terms, own, local_sem)
+    load.start()
+    summation.greet()
+    load.wait()
+    summation.begin()
+    for step in range(summation.steps):
+        summation.advance(step)
+
+
+def summed_over_devices(stacked):
+    rows, cols = lax.axis_size("row"), lax.axis_size("col")
+    devices = rows * cols
+    height, width = stacked.shape
+    chunk = -(-height // (16 * devices)) * 16
+    padded = jnp.pad(stacked, ((0, chunk * devices - height), (0, 0)))
+    halves = padded.reshape(devices, chunk, 2, width // 2).transpose(2, 0, 1, 3)
+    shape = halves.shape
+    count = Summation.semaphores(rows, cols)
+    summed = pl.pallas_call(
+        functools.partial(summation_kernel, rows, cols),
+        out_shape=jax.ShapeDtypeStruct(shape, jnp.bfloat16),
+        in_specs=[pl.BlockSpec(memory_space=pl.ANY)],
+        out_specs=pl.BlockSpec(memory_space=pltpu.VMEM),
+        scratch_shapes=[
+            pltpu.VMEM(shape, jnp.bfloat16),
+            pltpu.VMEM(shape, jnp.bfloat16),
+            pltpu.SemaphoreType.DMA((2, count)),
+            pltpu.SemaphoreType.DMA((2, count)),
+            pltpu.SemaphoreType.DMA,
+        ],
+        compiler_params=pltpu.CompilerParams(
+            collective_id=1, has_side_effects=True, vmem_limit_bytes=48 << 20
+        ),
+    )(halves)
+    return summed.transpose(1, 2, 0, 3).reshape(devices * chunk, width)[:height]
 
 
 def local(
@@ -144,8 +333,7 @@
     )
     sizes = [gradient.shape[0] for gradient in gradients]
     stacked = jnp.concatenate([low(gradient * scale) for gradient in gradients], axis=0)
-    share = lax.psum_scatter(stacked, ("row", "col"), scatter_dimension=0, tiled=True)
-    summed = lax.all_gather(share, ("row", "col"), axis=0, tiled=True).astype(jnp.float32)
+    summed = summed_over_devices(stacked).astype(jnp.float32)
     starts = [sum(sizes[:number]) for number in range(len(sizes))]
     totals = [
         lax.slice_in_dim(summed, start, start + size, axis=0)

time: 385 us -> 304 us (0.79); the launches traced: 384 us -> 299 us
  waiting for transfers between devices: 228 us -> 72.1 us
  Pallas kernels: 0 us -> 65.7 us
  blocking collectives: 29.7 us -> 0 us
  local copies, waits for them, and re-layouts: 14.1 us -> 42.8 us
  starting transfers between devices: 32.8 us -> 47.2 us
  between operations: 14.8 us -> 1.53 us
  other arithmetic: 0.83 us -> 4.72 us
    reduce_scatter x1 -> x0, waiting for transfers between devices: 138 us -> none  [local(): lax.psum_scatter(stacked, ('row', 'col'), scatter_dimension=0, tiled=True)]
    pallas_call x0 -> x1, Pallas kernels: none -> 65.7 us  [summed_over_devices(): pl.pallas_call(functools.partial(summation_kernel, rows, cols), out_shape...]
    all_to_all x1 -> x0, blocking collectives: 29.7 us -> none  [trade_slots(): lax.all_to_all(buffer, ('row', 'col'), split_axis=0, concat_axis=0, tiled...]
    all_gather x1 -> x0, waiting for transfers between devices: 22.4 us -> none  [local(): lax.all_gather(share, ('row', 'col'), axis=0, tiled=True)]
    convert_element_type x0 -> x1, local copies, waits for them, and re-layouts: none -> 11.9 us  [local(): summed = summed_over_devices(stacked).astype(jnp.float32)]
    reshape x0 -> x2, local copies, waits for them, and re-layouts: none -> 10.7 us  [summed_over_devices(): halves = padded.reshape(devices, chunk, 2, width // 2).transpose(2, 0, 1, 3)]
    ppermute x8, starting transfers between devices: 20 us -> 30.5 us  [passed_along(): lax.ppermute(value, axis, [(source, source + steps) for source in range(i...]
    unnamed x90 -> x91, local copies, waits for them, and re-layouts: 6.49 us -> 11.9 us
  transfers between devices with their start and end apart: 13 -> 12, of which waited for: 5 -> 3; matrix products, arithmetic and copies ran while one was open for 4% -> 26% of each run, Pallas kernels for 0% -> 22%
where the time goes in v2:
time: 304 us; the launch traced here: 299 us
  waiting for transfers between devices  72.1 us (24%)
  Pallas kernels  65.7 us (22%)
  matrix products  64.6 us (21%)
  starting transfers between devices  47.2 us (16%)
  local copies, waits for them, and re-layouts  42.8 us (14%)
  other arithmetic  4.72 us (2%)
    all_to_all x4, waiting for transfers between devices, trade_slots(): lax.all_to_all(buffer, ('row', 'col'), split_axis=0, concat_axis=0, tiled...  72.1 us
    pallas_call x1, Pallas kernels, summed_over_devices(): pl.pallas_call(functools.partial(summation_kernel, rows, cols), out_shape...  65.7 us
    ppermute x8, starting transfers between devices, passed_along(): lax.ppermute(value, axis, [(source, source + steps) for source in range(i...  30.5 us
    dot_general x13, matrix products, product(): return jnp.dot(first, second, preferred_element_type=jnp.float32)  29.6 us
    dot_general x14, matrix products, left_product(): lax.dot_general(first, second, (((0,), (0,)), ((), ())), preferred_elemen...  28.8 us
    all_to_all x4, starting transfers between devices, trade_slots(): lax.all_to_all(buffer, ('row', 'col'), split_axis=0, concat_axis=0, tiled...  16.7 us
    unnamed x91, local copies, waits for them, and re-layouts  11.9 us
    convert_element_type x1, local copies, waits for them, and re-layouts, local(): summed = summed_over_devices(stacked).astype(jnp.float32)  11.9 us
  transfers between devices with their start and end apart: 12, of which 3 were waited for; matrix products, arithmetic and copies ran while one was open for 26% of the time, Pallas kernels for 22%

profile of v2, /device:TPU:0, one launch (start us, length us, event | category | flops | bytes accessed | tf_op | source)
XLA Modules:
  0.0 298.7 jit_solution(16900846274867525925)
XLA Ops:
  0.6 0.9 eq.88
  1.5 1.3 convolution_convert_fusion.4
  2.8 1.3 collective-permute-start.3
  4.1 3.0 %collective-permute-start.2 = (bf16[32,512]{1,0:T(8,128)(2,1)S(1)}, bf16[32,512]{1,0:T(8,128)(2,1)S(1)}, u32[]{:S(2)}, u32[]{:S(2)}) collective-permute-start(bf16[32,512]{1,0:T(8,128)(2,1)S(1)} %get-tuple-element.18), channel_id=1, source_target_pairs={{0,1},{1,2},{2,3},{3,4},{4,5},{5,6},{6,7},{8,9},{9,10},{10,11},{11... | collective-permute-start | bytes 98312 | tf_op jit(solution)/shard_map/ppermute | solution.py:15
  7.2 1.3 collective-permute-start.1
  8.5 5.6 %collective-permute-start = (bf16[32,512]{1,0:T(8,128)(2,1)S(1)}, bf16[32,512]{1,0:T(8,128)(2,1)S(1)}, u32[]{:S(2)}, u32[]{:S(2)}) collective-permute-start(bf16[32,512]{1,0:T(8,128)(2,1)S(1)} %get-tuple-element.20), channel_id=1, source_target_pairs={{0,8},{8,16},{16,24},{1,9},{9,17},{17,25},{2,10},{10,18},{18,26},{... | collective-permute-start | bytes 98312 | tf_op jit(solution)/shard_map/ppermute | solution.py:15
  14.0 1.0 fusion.42
  15.1 0.7 convert_add_fusion
  15.8 1.1 constant_dynamic-update-slice_fusion.4
  16.8 1.3 copy.29
  18.3 5.6 %fusion.1 = f32[2048,512]{1,0:T(8,128)} fusion(s32[2048]{0:T(1024)} %param.15, bf16[640,512]{1,0:T(8,128)(2,1)S(1)} %constant_dynamic-update-slice_fusion, bf16[512,512]{1,0:T(8,128)(2,1)} %param.20), kind=kOutput, calls=%fused_computation.3 | convolution fusion | flops 1679360000 | bytes 5382144 | tf_op jit(solution)/shard_map/dot_general | solution.py:19
  23.8 5.8 %fusion.6 = f32[2048,512]{1,0:T(8,128)} fusion(f32[2048,512]{1,0:T(8,128)} %fusion.1, s32[2048]{0:T(1024)S(1)} %copy-done.21, bf16[512,512]{1,0:T(8,128)(2,1)S(1)} %copy-done.3, bf16[512,512]{1,0:T(8,128)(2,1)S(1)} %copy-done.8), kind=kOutput, calls=%fused_computation.16 | convolution fusion | flops 1344536576 | bytes 9445376 | tf_op jit(solution)/shard_map/dot_general | solution.py:19
  29.6 3.6 %fusion.73 = f32[2048,512]{1,0:T(8,128)S(1)} fusion(bf16[512,512]{1,0:T(8,128)(2,1)} %param.22, f32[2048,512]{1,0:T(8,128)} %fusion.6), kind=kOutput, calls=%fused_computation.123 | convolution fusion | flops 1078984704 | bytes 8912896 | tf_op jit(solution)/shard_map/dot_general | solution.py:19
  33.3 2.2 fusion.26
  35.5 0.7 fusion.47
  37.2 1.8 fusion.17
  39.0 5.3 %all-to-all-start = ((bf16[32,32,512]{2,1,0:T(8,128)(2,1)}), bf16[32,32,512]{2,1,0:T(8,128)(2,1)S(1)}, u32[]{:S(2)}, u32[]{:S(2)}) async-start(bf16[32,32,512]{2,1,0:T(8,128)(2,1)} %bitcast.64), calls=%async_computation | async-start | bytes 2097152 | tf_op jit(solution)/shard_map/all_to_all | solution.py:57
  44.4 2.8 fusion.18
  47.2 23.4 %all-to-all-done = bf16[32,32,512]{2,1,0:T(8,128)(2,1)S(1)} async-done(((bf16[32,32,512]{2,1,0:T(8,128)(2,1)}), bf16[32,32,512]{2,1,0:T(8,128)(2,1)S(1)}, u32[]{:S(2)}, u32[]{:S(2)}) %all-to-all-start) | async-done | bytes 1048608 | tf_op jit(solution)/shard_map/all_to_all | solution.py:57
  70.6 4.0 %all-to-all-start.2 = ((bf16[32,32,512]{2,1,0:T(8,128)(2,1)}), bf16[32,32,512]{2,1,0:T(8,128)(2,1)}, u32[]{:S(2)}, u32[]{:S(2)}) async-start(bf16[32,32,512]{2,1,0:T(8,128)(2,1)} %bitcast.62), calls=%async_computation.2 | async-start | bytes 2097152 | tf_op jit(solution)/shard_map/all_to_all | solution.py:57
  74.8 0.5 copy-done.29
  75.6 1.3 fusion.78
  76.9 23.9 %all-to-all-done.2 = bf16[32,32,512]{2,1,0:T(8,128)(2,1)} async-done(((bf16[32,32,512]{2,1,0:T(8,128)(2,1)}), bf16[32,32,512]{2,1,0:T(8,128)(2,1)}, u32[]{:S(2)}, u32[]{:S(2)}) %all-to-all-start.2) | async-done | bytes 1048608 | tf_op jit(solution)/shard_map/all_to_all | solution.py:57
  100.8 1.5 fusion.41
  102.4 2.8 convolution_convert_fusion
  105.2 3.6 %all-to-all-start.3 = ((bf16[32,32,512]{2,1,0:T(8,128)(2,1)}), bf16[32,32,512]{2,1,0:T(8,128)(2,1)S(1)}, u32[]{:S(2)}, u32[]{:S(2)}) async-start(bf16[32,32,512]{2,1,0:T(8,128)(2,1)} %bitcast.63), calls=%async_computation.3 | async-start | bytes 2097152 | tf_op jit(solution)/shard_map/all_to_all | solution.py:57
  108.8 1.5 convolution_convert_fusion.1
  110.3 24.8 %all-to-all-done.3 = bf16[32,32,512]{2,1,0:T(8,128)(2,1)S(1)} async-done(((bf16[32,32,512]{2,1,0:T(8,128)(2,1)}), bf16[32,32,512]{2,1,0:T(8,128)(2,1)S(1)}, u32[]{:S(2)}, u32[]{:S(2)}) %all-to-all-start.3) | async-done | bytes 1048608 | tf_op jit(solution)/shard_map/all_to_all | solution.py:57
  135.0 3.7 %all-to-all-start.1 = ((bf16[32,32,512]{2,1,0:T(8,128)(2,1)}), bf16[32,32,512]{2,1,0:T(8,128)(2,1)}, u32[]{:S(2)}, u32[]{:S(2)}) async-start(bf16[32,32,512]{2,1,0:T(8,128)(2,1)} %bitcast.3), calls=%async_computation.1 | async-start | bytes 2097152 | tf_op jit(solution)/shard_map/all_to_all | solution.py:57
  138.8 2.2 fusion.21
  141.1 0.6 fusion.31
  141.8 0.8 copy-done.14
  142.6 0.7 fusion.79
  143.3 1.3 copy-done.4
  144.6 2.8 multiply_convert_fusion.1
  147.5 2.4 multiply_convert_fusion
  149.9 1.7 fusion.27
  151.6 2.0 fusion.23
  153.6 0.5 fusion.77
  154.2 1.4 fusion.29
  155.6 1.3 fusion.38
  156.9 1.3 copy.31
  158.1 0.7 fusion.75
  158.8 1.3 collective-permute-start.4
  160.1 2.7 collective-permute-start.7
  162.8 1.3 collective-permute-start.6
  164.1 14.1 %collective-permute-start.5 = (bf16[32,512]{1,0:T(8,128)(2,1)}, bf16[32,512]{1,0:T(8,128)(2,1)}, u32[]{:S(2)}, u32[]{:S(2)}) collective-permute-start(bf16[32,512]{1,0:T(8,128)(2,1)} %get-tuple-element.16), channel_id=1, source_target_pairs={{0,8},{8,16},{16,24},{1,9},{9,17},{17,25},{2,10},{10,18},{18,26},{... | collective-permute-start | bytes 98312 | tf_op jit(solution)/shard_map/ppermute | solution.py:15
  178.1 0.8 constant_dynamic-update-slice_fusion.5
  178.9 5.1 %fusion.34 = bf16[3584,512]{1,0:T(8,128)(2,1)} fusion(bf16[3584,512]{1,0:T(8,128)(2,1)} %constant_dynamic-update-slice_fusion.5, bf16[2048,512]{1,0:T(8,128)(2,1)} %copy-done.41, f32[2048,512]{1,0:T(8,128)} %fusion.6), kind=kOutput, calls=%fused_computation.59 | convolution fusion | flops 1079508992 | bytes 6815744 | tf_op jit(solution)/shard_map/dot_general | solution.py:23
  184.1 1.7 fusion.19
  185.8 1.3 fusion.36
  187.1 1.1 fusion.25
  188.2 6.3 %reshape.56 = bf16[32,112,2,256]{3,2,1,0:T(2,128)(2,1)} reshape(bf16[3584,512]{1,0:T(8,128)(2,1)} %fusion.25) | data formatting | bytes 7340032 | tf_op jit(solution)/shard_map/reshape | solution.py:224
  194.5 4.4 %copy.37 = bf16[32,112,2,256]{3,1,0,2:T(8,128)(2,1)} copy(bf16[32,112,2,256]{3,2,1,0:T(2,128)(2,1)} %reshape.56) | data formatting | bytes 7340032 | tf_op jit(solution)/shard_map/reshape | solution.py:224
  198.9 65.7 %shard_map.188 = bf16[2,32,112,256]{3,2,1,0:T(8,128)(2,1)S(1)} custom-call(bf16[2,32,112,256]{3,2,1,0:T(8,128)(2,1)} %bitcast.59), custom_call_target="tpu_custom_call" | custom-call | tf_op jit(solution)/shard_map/pallas_call | solution.py:227
  264.6 3.9 %convert_bitcast_fusion = f32[32,112,2,256]{3,1,0,2:T(8,128)} fusion(bf16[2,32,112,256]{3,2,1,0:T(8,128)(2,1)S(1)} %shard_map.188), kind=kLoop, calls=%fused_computation | loop fusion | flops 1835008 | bytes 11010048 | tf_op jit(solution)/shard_map/convert_element_type | solution.py:336
  268.5 11.9 %copy.33 = f32[32,112,2,256]{3,2,1,0:T(2,128)} copy(f32[32,112,2,256]{3,1,0,2:T(8,128)} %convert_bitcast_fusion) | data formatting | bytes 14680064 | tf_op jit(solution)/shard_map/convert_element_type | solution.py:336
  280.4 4.1 %copy.35 = f32[448,8,2,256]{3,1,2,0:T(8,128)S(1)} copy(f32[448,8,2,256]{3,2,1,0:T(2,128)} %bitcast.58) | data formatting | bytes 14680064
  284.5 1.9 fusion.22
  286.4 1.4 copy-done.2
  287.8 2.4 fusion.74
  290.2 2.9 fusion.37
  293.2 3.1 %slice.97 = f32[1024,512]{1,0:T(8,128)} slice(f32[3584,512]{1,0:T(8,128)} %bitcast.57), slice={[1536:2560], [0:512]} | slice | bytes 4194304 | tf_op jit(solution)/shard_map/slice | solution.py:339
  296.3 2.2 convolution_add_fusion
  (98 shorter events, 1.7 us)
Async XLA Ops:
  0.6 34.8 %copy-start = (bf16[1024,512]{1,0:T(8,128)(2,1)S(1)}, bf16[1024,512]{1,0:T(8,128)(2,1)}, u32[]{:S(2)}) copy-start(bf16[1024,512]{1,0:T(8,128)(2,1)} %param.23) | copy-start | bytes 3145732
  2.8 15.4 %collective-permute-start.3 = (bf16[32,512]{1,0:T(8,128)(2,1)S(1)}, bf16[32,512]{1,0:T(8,128)(2,1)S(1)}, u32[]{:S(2)}, u32[]{:S(2)}) collective-permute-start(bf16[32,512]{1,0:T(8,128)(2,1)S(1)} %get-tuple-element.17), channel_id=1, source_target_pairs={{1,0},{2,1},{3,2},{4,3},{5,4},{6,5},{7,6},{9,8},{10,9},{11,10},{12... | collective-permute-start | bytes 98312 | tf_op jit(solution)/shard_map/ppermute | solution.py:15
  4.1 14.0 %collective-permute-start.2 = (bf16[32,512]{1,0:T(8,128)(2,1)S(1)}, bf16[32,512]{1,0:T(8,128)(2,1)S(1)}, u32[]{:S(2)}, u32[]{:S(2)}) collective-permute-start(bf16[32,512]{1,0:T(8,128)(2,1)S(1)} %get-tuple-element.18), channel_id=1, source_target_pairs={{0,1},{1,2},{2,3},{3,4},{4,5},{5,6},{6,7},{8,9},{9,10},{10,11},{11... | collective-permute-start | bytes 98312 | tf_op jit(solution)/shard_map/ppermute | solution.py:15
  7.2 11.0 %collective-permute-start.1 = (bf16[32,512]{1,0:T(8,128)(2,1)S(1)}, bf16[32,512]{1,0:T(8,128)(2,1)S(1)}, u32[]{:S(2)}, u32[]{:S(2)}) collective-permute-start(bf16[32,512]{1,0:T(8,128)(2,1)S(1)} %get-tuple-element.19), channel_id=1, source_target_pairs={{8,0},{16,8},{24,16},{9,1},{17,9},{25,17},{10,2},{18,10},{26,18},{... | collective-permute-start | bytes 98312 | tf_op jit(solution)/shard_map/ppermute | solution.py:15
  8.5 9.6 %collective-permute-start = (bf16[32,512]{1,0:T(8,128)(2,1)S(1)}, bf16[32,512]{1,0:T(8,128)(2,1)S(1)}, u32[]{:S(2)}, u32[]{:S(2)}) collective-permute-start(bf16[32,512]{1,0:T(8,128)(2,1)S(1)} %get-tuple-element.20), channel_id=1, source_target_pairs={{0,8},{8,16},{16,24},{1,9},{9,17},{17,25},{2,10},{10,18},{18,26},{... | collective-permute-start | bytes 98312 | tf_op jit(solution)/shard_map/ppermute | solution.py:15
  15.8 28.6 %copy-start.23 = (s32[512]{0:T(512)}, s32[512]{0:T(512)S(1)}, u32[]{:S(2)}) copy-start(s32[512]{0:T(512)S(1)} %convert_add_fusion) | copy-start | bytes 6148
  18.1 17.3 %copy-start.16 = (bf16[512,512]{0,1:T(8,128)(2,1)}, bf16[512,512]{0,1:T(8,128)(2,1)S(1)}, u32[]{:S(2)}) copy-start(bf16[512,512]{0,1:T(8,128)(2,1)S(1)} %copy.29) | copy-start | bytes 1572868
  18.2 5.6 %copy-start.19 = (bf16[640,512]{1,0:T(8,128)(2,1)}, bf16[640,512]{1,0:T(8,128)(2,1)S(1)}, u32[]{:S(2)}) copy-start(bf16[640,512]{1,0:T(8,128)(2,1)S(1)} %constant_dynamic-update-slice_fusion) | copy-start | bytes 1966084
  18.2 5.6 %copy-start.3 = (bf16[512,512]{1,0:T(8,128)(2,1)S(1)}, bf16[512,512]{1,0:T(8,128)(2,1)}, u32[]{:S(2)}) copy-start(bf16[512,512]{1,0:T(8,128)(2,1)} %param.13) | copy-start | bytes 1572868
  18.2 5.6 %copy-start.8 = (bf16[512,512]{1,0:T(8,128)(2,1)S(1)}, bf16[512,512]{1,0:T(8,128)(2,1)}, u32[]{:S(2)}) copy-start(bf16[512,512]{1,0:T(8,128)(2,1)} %param.21) | copy-start | bytes 1572868
  18.2 5.6 %copy-start.21 = (s32[2048]{0:T(1024)S(1)}, s32[2048]{0:T(1024)}, u32[]{:S(2)}) copy-start(s32[2048]{0:T(1024)} %param.16) | copy-start | bytes 24580
  33.3 2.2 copy-start.39
  35.5 1.7 copy-start.37
  35.5 1.2 copy-start.25
  36.7 2.3 copy-start.34
  37.2 1.8 copy-start.32
  39.0 35.6 %copy-start.22 = (s32[1,1024]{1,0:T(1,128)S(1)}, s32[1,1024]{1,0:T(1,128)}, u32[]{:S(2)}) copy-start(s32[1,1024]{1,0:T(1,128)} %param.19) | copy-start | bytes 12292
  39.0 31.6 %all-to-all-start = ((bf16[32,32,512]{2,1,0:T(8,128)(2,1)}), bf16[32,32,512]{2,1,0:T(8,128)(2,1)S(1)}, u32[]{:S(2)}, u32[]{:S(2)}) async-start(bf16[32,32,512]{2,1,0:T(8,128)(2,1)} %bitcast.64), calls=%async_computation | async-start | bytes 2097152 | tf_op jit(solution)/shard_map/all_to_all | solution.py:57
  70.6 30.2 %all-to-all-start.2 = ((bf16[32,32,512]{2,1,0:T(8,128)(2,1)}), bf16[32,32,512]{2,1,0:T(8,128)(2,1)}, u32[]{:S(2)}, u32[]{:S(2)}) async-start(bf16[32,32,512]{2,1,0:T(8,128)(2,1)} %bitcast.62), calls=%async_computation.2 | async-start | bytes 2097152 | tf_op jit(solution)/shard_map/all_to_all | solution.py:57
  74.8 0.5 copy-start.29
  102.4 2.8 copy-start.30
  105.2 29.9 %all-to-all-start.3 = ((bf16[32,32,512]{2,1,0:T(8,128)(2,1)}), bf16[32,32,512]{2,1,0:T(8,128)(2,1)S(1)}, u32[]{:S(2)}, u32[]{:S(2)}) async-start(bf16[32,32,512]{2,1,0:T(8,128)(2,1)} %bitcast.63), calls=%async_computation.3 | async-start | bytes 2097152 | tf_op jit(solution)/shard_map/all_to_all | solution.py:57
  135.0 3.8 %copy-start.11 = (bf16[32,32,512]{2,1,0:T(8,128)(2,1)}, bf16[32,32,512]{2,1,0:T(8,128)(2,1)S(1)}, u32[]{:S(2)}) copy-start(bf16[32,32,512]{2,1,0:T(8,128)(2,1)S(1)} %all-to-all-done.3) | copy-start | bytes 3145732
  135.0 155.2 %all-to-all-start.1 = ((bf16[32,32,512]{2,1,0:T(8,128)(2,1)}), bf16[32,32,512]{2,1,0:T(8,128)(2,1)}, u32[]{:S(2)}, u32[]{:S(2)}) async-start(bf16[32,32,512]{2,1,0:T(8,128)(2,1)} %bitcast.3), calls=%async_computation.1 | async-start | bytes 2097152 | tf_op jit(solution)/shard_map/all_to_all | solution.py:57
  138.8 2.3 copy-start.26
  138.8 2.3 copy-start.35
  141.1 2.2 copy-start.9
  141.1 3.5 %copy-start.40 = (f32[2048,512]{1,0:T(8,128)S(1)}, f32[2048,512]{1,0:T(8,128)}, u32[]{:S(2)}) copy-start(f32[2048,512]{1,0:T(8,128)} %copy-done.39) | copy-start | bytes 12582916
  141.8 0.8 copy-start.14
  143.3 1.3 copy-start.4
  144.6 2.9 copy-start.7
  144.6 2.9 copy-start.27
  147.5 2.4 copy-start.41
  149.9 1.7 copy-start.28
  151.6 4.0 %copy-start.12 = (bf16[512,512]{1,0:T(8,128)(2,1)}, bf16[512,512]{1,0:T(8,128)(2,1)S(1)}, u32[]{:S(2)}) copy-start(bf16[512,512]{1,0:T(8,128)(2,1)S(1)} %fusion.27) | copy-start | bytes 1572868
  151.6 2.0 copy-start.18
  151.6 2.5 copy-start.20
  158.8 137.5 %collective-permute-start.4 = (bf16[32,512]{1,0:T(8,128)(2,1)}, bf16[32,512]{1,0:T(8,128)(2,1)}, u32[]{:S(2)}, u32[]{:S(2)}) collective-permute-start(bf16[32,512]{1,0:T(8,128)(2,1)} %get-tuple-element.13), channel_id=1, source_target_pairs={{8,0},{16,8},{24,16},{9,1},{17,9},{25,17},{10,2},{18,10},{26,18},{... | collective-permute-start | bytes 98312 | tf_op jit(solution)/shard_map/ppermute | solution.py:15
  160.1 136.2 %collective-permute-start.7 = (bf16[32,512]{1,0:T(8,128)(2,1)}, bf16[32,512]{1,0:T(8,128)(2,1)}, u32[]{:S(2)}, u32[]{:S(2)}) collective-permute-start(bf16[32,512]{1,0:T(8,128)(2,1)} %get-tuple-element.14), channel_id=1, source_target_pairs={{0,1},{1,2},{2,3},{3,4},{4,5},{5,6},{6,7},{8,9},{9,10},{10,11},{11... | collective-permute-start | bytes 98312 | tf_op jit(solution)/shard_map/ppermute | solution.py:15
  162.8 133.5 %collective-permute-start.6 = (bf16[32,512]{1,0:T(8,128)(2,1)}, bf16[32,512]{1,0:T(8,128)(2,1)}, u32[]{:S(2)}, u32[]{:S(2)}) collective-permute-start(bf16[32,512]{1,0:T(8,128)(2,1)} %get-tuple-element.15), channel_id=1, source_target_pairs={{1,0},{2,1},{3,2},{4,3},{5,4},{6,5},{7,6},{9,8},{10,9},{11,10},{12... | collective-permute-start | bytes 98312 | tf_op jit(solution)/shard_map/ppermute | solution.py:15
  164.1 132.2 %collective-permute-start.5 = (bf16[32,512]{1,0:T(8,128)(2,1)}, bf16[32,512]{1,0:T(8,128)(2,1)}, u32[]{:S(2)}, u32[]{:S(2)}) collective-permute-start(bf16[32,512]{1,0:T(8,128)(2,1)} %get-tuple-element.16), channel_id=1, source_target_pairs={{0,8},{8,16},{16,24},{1,9},{9,17},{17,25},{2,10},{10,18},{18,26},{... | collective-permute-start | bytes 98312 | tf_op jit(solution)/shard_map/ppermute | solution.py:15
  178.9 5.1 %copy-start.15 = (bf16[512,512]{1,0:T(8,128)(2,1)S(1)}, bf16[512,512]{1,0:T(8,128)(2,1)}, u32[]{:S(2)}) copy-start(bf16[512,512]{1,0:T(8,128)(2,1)} %copy-done.14) | copy-start | bytes 1572868
  178.9 5.1 %copy-start.17 = (bf16[512,512]{0,1:T(8,128)(2,1)S(1)}, bf16[512,512]{0,1:T(8,128)(2,1)}, u32[]{:S(2)}) copy-start(bf16[512,512]{0,1:T(8,128)(2,1)} %copy-done.16) | copy-start | bytes 1572868
  178.9 5.1 %copy-start.38 = (bf16[512,512]{0,1:T(8,128)(2,1)S(1)}, bf16[512,512]{0,1:T(8,128)(2,1)}, u32[]{:S(2)}) copy-start(bf16[512,512]{0,1:T(8,128)(2,1)} %copy-done.37) | copy-start | bytes 1572868
  184.1 1.7 copy-start.10
  184.1 1.7 copy-start.36
  185.8 1.3 copy-start.31
  280.4 4.1 %copy-start.5 = (f32[512,1024]{1,0:T(8,128)S(1)}, f32[512,1024]{1,0:T(8,128)}, u32[]{:S(2)}) copy-start(f32[512,1024]{1,0:T(8,128)} %copy-done.4) | copy-start | bytes 6291460
  280.4 4.1 %copy-start.13 = (bf16[512,512]{1,0:T(8,128)(2,1)S(1)}, bf16[512,512]{1,0:T(8,128)(2,1)}, u32[]{:S(2)}) copy-start(bf16[512,512]{1,0:T(8,128)(2,1)} %copy-done.12) | copy-start | bytes 1572868
  284.5 3.3 %copy-start.2 = (f32[448,8,2,256]{3,1,2,0:T(8,128)}, f32[448,8,2,256]{3,1,2,0:T(8,128)S(1)}, u32[]{:S(2)}) copy-start(f32[448,8,2,256]{3,1,2,0:T(8,128)S(1)} %copy.35) | copy-start | bytes 22020100
  287.8 2.4 copy-start.24
  287.8 2.4 copy-start.33
  290.2 6.0 %copy-start.6 = (f32[512,512]{1,0:T(8,128)S(1)}, f32[512,512]{1,0:T(8,128)}, u32[]{:S(2)}) copy-start(f32[512,512]{1,0:T(8,128)} %fusion.22) | copy-start | bytes 3145732
  290.2 8.2 %copy-start.1 = (bf16[1024,512]{1,0:T(8,128)(2,1)S(1)}, bf16[1024,512]{1,0:T(8,128)(2,1)}, u32[]{:S(2)}) copy-start(bf16[1024,512]{1,0:T(8,128)(2,1)} %param.23) | copy-start | bytes 3145732

commit v3 on v2

--- a/solution.py
+++ b/solution.py
@@ -193,54 +193,270 @@
             if step + 1 < self.steps:
                 self.start(half, step + 1)
 
-    def greet(self):
-        barrier = pltpu.get_barrier_semaphore()
-        peers = [(self.row, self.across(bit)) for bit in range(self.bits)]
-        peers += [(self.along(ahead), self.col) for ahead in range(1, self.rows)]
-        for peer in peers:
-            pl.semaphore_signal(
-                barrier, inc=1, device_id=peer, device_id_type=pl.DeviceIdType.MESH
+
+def hot_rows(column, count):
+    spread = lax.broadcasted_iota(jnp.int32, (column.shape[0], count), 1)
+    return jnp.where(spread == column, 1.0, 0.0).astype(jnp.bfloat16)
+
+
+def hot_columns(row, count):
+    spread = lax.broadcasted_iota(jnp.int32, (count, row.shape[1]), 0)
+    return jnp.where(spread == row, 1.0, 0.0).astype(jnp.bfloat16)
+
+
+def sigmoid(value):
+    return 1.0 / (1.0 + jnp.exp(-value))
+
+
+def slope(value):
+    sigma = sigmoid(value)
+    return sigma * (1.0 + value * (1.0 - sigma))
+
+
+def forward_kernel(
+    block,
+    nodes,
+    halo,
+    source_column,
+    target_column,
+    target_row,
+    slot_row,
+    source_weight,
+    target_weight,
+    edge_weight,
+    inner_weight,
+    outer_weight,
+    edge_linear,
+    edge_hidden,
+    message_linear,
+    aggregate,
+    node_linear,
+    node_hidden,
+    refined,
+    slots,
+    sides,
+    sums,
+):
+    count_rows, width = nodes.shape
+    own = nodes[...]
+    extra = halo.shape[0]
+    sides[0:count_rows, :] = low(product(own, source_weight[...]))
+    sides[count_rows : count_rows + extra, :] = low(product(halo[...], source_weight[...]))
+    sides[count_rows + extra :, :] = low(product(own, target_weight[...]))
+    sums[...] = jnp.zeros_like(sums)
+
+    @pl.loop(0, edge_linear.shape[0] // block)
+    def _(number):
+        here = pl.ds(pl.multiple_of(number * block, block), block)
+        linear = product(
+            hot_rows(source_column[here, :], count_rows + extra), sides[0 : count_rows + extra, :]
+        )
+        linear += product(hot_rows(target_column[here, :], count_rows), sides[count_rows + extra :, :])
+        edge_linear[here, :] = low(linear)
+        hidden = low(linear * sigmoid(linear))
+        edge_hidden[here, :] = hidden
+        message = product(hidden, edge_weight[...])
+        message_linear[here, :] = low(message)
+        sums[...] += product(
+            hot_columns(target_row[number], count_rows), low(message * sigmoid(message))
+        )
+
+    gathered = low(sums[...])
+    aggregate[...] = gathered
+    linear = product(own, inner_weight[0:width, :]) + product(gathered, inner_weight[width:, :])
+    node_linear[...] = linear
+    hidden = low(linear * sigmoid(linear))
+    node_hidden[...] = hidden
+    result = low(own.astype(jnp.float32) + product(hidden, outer_weight[...]))
+    refined[...] = result
+    places = slots.shape[0]
+    step = count_rows
+    for start in range(0, places, step):
+        spread = lax.broadcasted_iota(jnp.int32, (step, count_rows), 0) + start
+        hot = jnp.where(spread == slot_row[...], 1.0, 0.0).astype(jnp.bfloat16)
+        slots[start : start + step, :] = low(product(hot, result))
+
+
+def pack(flat, own):
+    chunk, half_width = own.shape[2:]
+
+    def move(number, carry):
+        for half in range(2):
+            own[half, number] = flat[
+                pl.ds(pl.multiple_of(number * chunk, 16), chunk),
+                half * half_width : (half + 1) * half_width,
+            ]
+        return carry
+
+    lax.fori_loop(0, own.shape[1], move, 0)
+
+
+def unpack(out, flat):
+    chunk, half_width = out.shape[2:]
+
+    def move(number, carry):
+        for half in range(2):
+            flat[
+                pl.ds(pl.multiple_of(number * chunk, 16), chunk),
+                half * half_width : (half + 1) * half_width,
+            ] = out[half, number]
+        return carry
+
+    lax.fori_loop(0, out.shape[1], move, 0)
+
+
+def backward_kernel(
+    rows,
+    cols,
+    block,
+    scale,
+    nodes,
+    halo,
+    cotangent,
+    shares,
+    slot_column,
+    target_column,
+    source_row,
+    target_row,
+    list_row,
+    coarse,
+    grad_coarse,
+    source_weight,
+    target_weight,
+    edge_weight,
+    inner_weight,
+    outer_weight,
+    edge_linear,
+    edge_hidden,
+    message_linear,
+    aggregate,
+    node_linear,
+    node_hidden,
+    node_gradient,
+    early_sums,
+    late_sums,
+    early_flat,
+    late_flat,
+    early_own,
+    early_land,
+    early_out,
+    late_own,
+    late_land,
+    late_out,
+    grad_aggregate,
+    source_sums,
+    target_sums,
+    edge_sums,
+    blocks,
+    landed,
+    early_send,
+    early_recv,
+    late_send,
+    late_recv,
+    halo_send,
+    halo_recv,
+):
+    early = Summation(rows, cols, early_own, early_land, early_out, early_send, early_recv)
+    late = Summation(rows, cols, late_own, late_land, late_out, late_send, late_recv)
+    row, col = early.row, early.col
+    neighbours = [
+        (lax.rem(row + rows - 1, jnp.int32(rows)), col),
+        (lax.rem(row + 1, jnp.int32(rows)), col),
+        (row, lax.rem(col + cols - 1, jnp.int32(cols))),
+        (row, lax.rem(col + 1, jnp.int32(cols))),
+    ]
+    barrier = pltpu.get_barrier_semaphore()
+    peers = [(row, early.across(bit)) for bit in range(early.bits)]
+    peers += [(early.along(ahead), col) for ahead in range(1, rows)]
+    peers += neighbours[2:]
+    for peer in peers:
+        pl.semaphore_signal(barrier, inc=1, device_id=peer, device_id_type=pl.DeviceIdType.MESH)
+
+    count_rows, width = nodes.shape
+    extra = halo.shape[0]
+    each = extra // 4
+    own = nodes[...]
+    share_rows = product(hot_rows(slot_column[...], shares.shape[0]), shares[...])
+    grad_refined = cotangent[...].astype(jnp.float32) + share_rows
+    refined_low = low(grad_refined)
+    early_flat[0:width, :] = low(scale * left_product(coarse[...], grad_coarse[...]))
+    early_flat[width : 2 * width, :] = low(scale * left_product(node_hidden[...], refined_low))
+    grad_hidden = low(right_product(refined_low, outer_weight[...]) * slope(node_linear[...]))
+    early_flat[2 * width : 3 * width, :] = low(scale * left_product(own, grad_hidden))
+    early_flat[3 * width : 4 * width, :] = low(scale * left_product(aggregate[...], grad_hidden))
+    pack(early_flat, early_own)
+    pl.semaphore_wait(barrier, len(peers))
+    early.begin()
+    grad_aggregate[...] = low(right_product(grad_hidden, inner_weight[width:, :]))
+    node_gradient[...] = grad_refined + right_product(grad_hidden, inner_weight[0:width, :])
+    source_sums[...] = jnp.zeros_like(source_sums)
+    target_sums[...] = jnp.zeros_like(target_sums)
+    edge_sums[...] = jnp.zeros_like(edge_sums)
+
+    for number in range(edge_linear.shape[0] // block):
+        here = pl.ds(number * block, block)
+        picked = product(hot_rows(target_column[here, :], count_rows), grad_aggregate[...])
+        grad_message = low(picked * slope(message_linear[here, :].astype(jnp.float32)))
+        edge_sums[...] += left_product(edge_hidden[here, :], grad_message)
+        grad_edges = low(
+            right_product(grad_message, edge_weight[...])
+            * slope(edge_linear[here, :].astype(jnp.float32))
+        )
+        source_sums[...] += product(hot_columns(source_row[number], count_rows + extra), grad_edges)
+        target_sums[...] += product(hot_columns(target_row[number], count_rows), grad_edges)
+        if number < early.steps:
+            early.advance(number)
+    done = min(edge_linear.shape[0] // block, early.steps)
+
+    grad_sources = low(source_sums[...])
+    grad_targets = low(target_sums[...])
+    blocks[...] = low(right_product(grad_sources[count_rows:], source_weight[...]))
+    returns = []
+    for number in range(4):
+        here = pl.ds(number * each, each)
+        returns.append(
+            pltpu.make_async_remote_copy(
+                src_ref=blocks.at[here],
+                dst_ref=landed.at[here],
+                send_sem=halo_send.at[number],
+                recv_sem=halo_recv.at[number],
+                device_id=neighbours[number],
+                device_id_type=pl.DeviceIdType.MESH,
             )
-        pl.semaphore_wait(barrier, len(peers))
-
-
-def summation_kernel(rows, cols, terms, out, own, land, send, recv, local_sem):
-    summation = Summation(rows, cols, own, land, out, send, recv)
-    load = pltpu.make_async_copy(terms, own, local_sem)
-    load.start()
-    summation.greet()
-    load.wait()
-    summation.begin()
-    for step in range(summation.steps):
-        summation.advance(step)
-
-
-def summed_over_devices(stacked):
-    rows, cols = lax.axis_size("row"), lax.axis_size("col")
-    devices = rows * cols
-    height, width = stacked.shape
-    chunk = -(-height // (16 * devices)) * 16
-    padded = jnp.pad(stacked, ((0, chunk * devices - height), (0, 0)))
-    halves = padded.reshape(devices, chunk, 2, width // 2).transpose(2, 0, 1, 3)
-    shape = halves.shape
-    count = Summation.semaphores(rows, cols)
-    summed = pl.pallas_call(
-        functools.partial(summation_kernel, rows, cols),
-        out_shape=jax.ShapeDtypeStruct(shape, jnp.bfloat16),
-        in_specs=[pl.BlockSpec(memory_space=pl.ANY)],
-        out_specs=pl.BlockSpec(memory_space=pltpu.VMEM),
-        scratch_shapes=[
-            pltpu.VMEM(shape, jnp.bfloat16),
-            pltpu.VMEM(shape, jnp.bfloat16),
-            pltpu.SemaphoreType.DMA((2, count)),
-            pltpu.SemaphoreType.DMA((2, count)),
-            pltpu.SemaphoreType.DMA,
-        ],
-        compiler_params=pltpu.CompilerParams(
-            collective_id=1, has_side_effects=True, vmem_limit_bytes=48 << 20
-        ),
-    )(halves)
-    return summed.transpose(1, 2, 0, 3).reshape(devices * chunk, width)[:height]
+        )
+    for copy in returns:
+        copy.start()
+    if late_flat.shape[0] > 3 * width:
+        late_flat[3 * width :, :] = jnp.zeros_like(late_flat[3 * width :, :])
+    late_flat[0:width, :] = low(
+        scale
+        * (
+            left_product(own, grad_sources[:count_rows])
+            + left_product(halo[...], grad_sources[count_rows:])
+        )
+    )
+    late_flat[width : 2 * width, :] = low(scale * left_product(own, grad_targets))
+    late_flat[2 * width : 3 * width, :] = low(scale * edge_sums[...])
+    pack(late_flat, late_own)
+    late.begin()
+    node_gradient[...] += right_product(grad_targets, target_weight[...]) + right_product(
+        grad_sources[:count_rows], source_weight[...]
+    )
+    for copy in returns:
+        copy.wait()
+    inside = [row + 1 < rows, row > 0, col + 1 < cols, col > 0]
+    for number in range(4):
+        here = pl.ds(number * each, each)
+        keep = jnp.where(inside[number], 1.0, 0.0).astype(jnp.bfloat16)
+        landed[here, :] = landed[here, :] * keep
+    node_gradient[...] += product(hot_columns(list_row[...], count_rows), landed[...])
+    for step in range(late.steps):
+        if done + step < early.steps:
+            early.advance(done + step)
+            if done + step == early.steps - 1:
+                unpack(early_out, early_sums)
+        late.advance(step)
+    unpack(late_out, late_sums)
 
 
 def local(
@@ -288,68 +504,134 @@
     picked = low(product(list_hot, nodes)).reshape(4, halo_rows, width)
     received = trade_halo([picked[number] for number in range(4)], 1)
     pooled_cotangent = toward_owners(cotangent)
-    extended = jnp.concatenate([nodes] + received, axis=0)
-    source_hot = one_hot(edge_source, extended.shape[0])
-    target_hot = one_hot(edge_target, count_rows)
-    source_side = low(product(extended, source_weight))
-    target_side = low(product(nodes, target_weight))
-    edge_linear = product(source_hot, source_side) + product(target_hot, target_side)
-    edge_hidden = low(jax.nn.silu(edge_linear))
-    message_linear = product(edge_hidden, edge_weight)
-    aggregate = low(left_product(target_hot, low(jax.nn.silu(message_linear))))
-    joined = jnp.concatenate([nodes, aggregate], axis=1)
-    node_linear = product(joined, inner_weight)
-    node_hidden = low(jax.nn.silu(node_linear))
-    refined = low(nodes.astype(jnp.float32) + product(node_hidden, outer_weight))
-    coarse = low(toward_owners(refined) / count)
+    halo = jnp.concatenate(received, axis=0)
+    edges = edge_source.shape[0]
+    block = math.gcd(512, edges)
+    source_column, target_column = edge_source[:, None], edge_target[:, None]
+    source_row = edge_source.reshape(edges // block, 1, block)
+    target_row = edge_target.reshape(edges // block, 1, block)
+    shaped = jax.ShapeDtypeStruct
+    whole = pl.BlockSpec(memory_space=pltpu.VMEM)
+    (
+        edge_linear,
+        edge_hidden,
+        message_linear,
+        aggregate,
+        node_linear,
+        node_hidden,
+        refined,
+        refined_slots,
+    ) = pl.pallas_call(
+        functools.partial(forward_kernel, block),
+        out_shape=(
+            shaped((edges, width), jnp.bfloat16),
+            shaped((edges, width), jnp.bfloat16),
+            shaped((edges, width), jnp.bfloat16),
+            shaped((count_rows, width), jnp.bfloat16),
+            shaped((count_rows, width), jnp.float32),
+            shaped((count_rows, width), jnp.bfloat16),
+            shaped((count_rows, width), jnp.bfloat16),
+            shaped((devices * capacity, width), jnp.bfloat16),
+        ),
+        in_specs=[whole] * 11,
+        out_specs=[whole] * 8,
+        scratch_shapes=[
+            pltpu.VMEM((2 * count_rows + 4 * halo_rows, width), jnp.bfloat16),
+            pltpu.VMEM((count_rows, width), jnp.float32),
+        ],
+        compiler_params=pltpu.CompilerParams(vmem_limit_bytes=40 << 20),
+        cost_estimate=pl.CostEstimate(
+            flops=6 * edges * width * width * 2, bytes_accessed=16 << 20, transcendentals=0
+        ),
+    )(
+        nodes,
+        halo,
+        source_column,
+        target_column,
+        target_row,
+        slot[None, :],
+        source_weight,
+        target_weight,
+        edge_weight,
+        inner_weight,
+        outer_weight,
+    )
+    coarse = low(product(member, trade_slots(refined_slots)) / count)
     coarse_linear = product(coarse, coarse_weight)
     coarse_update = low(jax.nn.silu(coarse_linear))
     grad_coarse = low(pooled_cotangent * silu_slope(coarse_linear))
     coarse_share = low(right_product(grad_coarse, coarse_weight) / count)
-    share_rows = toward_sources(coarse_share)
+    shares = trade_slots(low(left_product(member, coarse_share)))
+    rows, cols = lax.axis_size("row"), lax.axis_size("col")
+    semaphores = Summation.semaphores(rows, cols)
+    heights = (4 * width, 3 * width)
+    chunks = [-(-height // (16 * devices)) * 16 for height in heights]
+    flats = [(devices * chunk, width) for chunk in chunks]
+    cuts = [(2, devices, chunk, width // 2) for chunk in chunks]
+    node_gradient, early_sums, late_sums = pl.pallas_call(
+        functools.partial(backward_kernel, rows, cols, block, scale),
+        out_shape=(
+            shaped((count_rows, width), jnp.float32),
+            shaped(flats[0], jnp.bfloat16),
+            shaped(flats[1], jnp.bfloat16),
+        ),
+        in_specs=[whole] * 22,
+        out_specs=[whole] * 3,
+        scratch_shapes=[pltpu.VMEM(flat, jnp.bfloat16) for flat in flats]
+        + [pltpu.VMEM(cuts[0], jnp.bfloat16)] * 3
+        + [pltpu.VMEM(cuts[1], jnp.bfloat16)] * 3
+        + [
+            pltpu.VMEM((count_rows, width), jnp.bfloat16),
+            pltpu.VMEM((count_rows + 4 * halo_rows, width), jnp.float32),
+            pltpu.VMEM((count_rows, width), jnp.float32),
+            pltpu.VMEM((width, width), jnp.float32),
+            pltpu.VMEM((4 * halo_rows, width), jnp.bfloat16),
+            pltpu.VMEM((4 * halo_rows, width), jnp.bfloat16),
+        ]
+        + [pltpu.SemaphoreType.DMA((2, semaphores))] * 4
+        + [pltpu.SemaphoreType.DMA((4,))] * 2,
+        compiler_params=pltpu.CompilerParams(
+            collective_id=1, has_side_effects=True, vmem_limit_bytes=56 << 20
+        ),
+        cost_estimate=pl.CostEstimate(
+            flops=8 * edges * width * width * 2, bytes_accessed=24 << 20, transcendentals=0
+        ),
+    )(
+        nodes,
+        halo,
+        cotangent,
+        shares.reshape(devices * capacity, width),
+        slot[:, None],
+        target_column,
+        source_row,
+        target_row,
+        all_lists[None, :],
+        coarse,
+        grad_coarse,
+        source_weight,
+        target_weight,
+        edge_weight,
+        inner_weight,
+        outer_weight,
+        edge_linear,
+        edge_hidden,
+        message_linear,
+        aggregate,
+        node_linear,
+        node_hidden,
+    )
     updated = low(refined.astype(jnp.float32) + toward_sources(coarse_update))
-    coarse_gradient = left_product(coarse, grad_coarse)
-    grad_refined = cotangent.astype(jnp.float32) + share_rows
-    refined_low = low(grad_refined)
-    outer_gradient = left_product(node_hidden, refined_low)
-    grad_hidden = low(right_product(refined_low, outer_weight) * silu_slope(node_linear))
-    inner_gradient = left_product(joined, grad_hidden)
-    grad_joined = right_product(grad_hidden, inner_weight)
-    grad_aggregate = low(grad_joined[:, width:])
-    grad_message = low(product(target_hot, grad_aggregate) * silu_slope(message_linear))
-    edge_gradient = left_product(edge_hidden, grad_message)
-    grad_edges = low(right_product(grad_message, edge_weight) * silu_slope(edge_linear))
-    grad_sources = low(left_product(source_hot, grad_edges))
-    grad_targets = low(left_product(target_hot, grad_edges))
-    source_gradient = left_product(extended, grad_sources)
-    target_gradient = left_product(nodes, grad_targets)
-    gradients = (
-        source_gradient,
-        target_gradient,
-        edge_gradient,
-        inner_gradient,
-        outer_gradient,
-        coarse_gradient,
-    )
-    sizes = [gradient.shape[0] for gradient in gradients]
-    stacked = jnp.concatenate([low(gradient * scale) for gradient in gradients], axis=0)
-    summed = summed_over_devices(stacked).astype(jnp.float32)
-    starts = [sum(sizes[:number]) for number in range(len(sizes))]
-    totals = [
-        lax.slice_in_dim(summed, start, start + size, axis=0)
-        for start, size in zip(starts, sizes)
-    ]
-    grad_extended = right_product(grad_sources, source_weight)
-    back_blocks = low(grad_extended[count_rows:]).reshape(4, halo_rows, width)
-    returned = trade_halo([back_blocks[number] for number in range(4)], -1)
-    node_gradient = (
-        grad_refined
-        + grad_joined[:, :width]
-        + right_product(grad_targets, target_weight)
-        + grad_extended[:count_rows]
-        + left_product(list_hot, jnp.concatenate(returned, axis=0))
-    )
-    return (updated, node_gradient, *totals)
+    early_sums, late_sums = early_sums.astype(jnp.float32), late_sums.astype(jnp.float32)
+    return (
+        updated,
+        node_gradient,
+        late_sums[:width],
+        late_sums[width : 2 * width],
+        late_sums[2 * width : 3 * width],
+        early_sums[2 * width : 4 * width],
+        early_sums[width : 2 * width],
+        early_sums[:width],
+    )
 
 
 def solution(mesh):

time: 304 us -> 247 us (0.81); the launches traced: 299 us -> 246 us
  matrix products: 64.6 us -> 10.2 us
  waiting for transfers between devices: 72.1 us -> 95.2 us
  Pallas kernels: 65.7 us -> 86.5 us
  starting transfers between devices: 47.2 us -> 27.6 us
  local copies, waits for them, and re-layouts: 42.8 us -> 24.1 us
    dot_general x13 -> x6, matrix products: 29.6 us -> 5.18 us  [product(): return jnp.dot(first, second, preferred_element_type=jnp.float32)]
    dot_general x14 -> x3, matrix products: 28.8 us -> 4.98 us  [left_product(): lax.dot_general(first, second, (((0,), (0,)), ((), ())), preferred_elemen...]
    all_to_all x4, waiting for transfers between devices: 72.1 us -> 95.2 us  [trade_slots(): lax.all_to_all(buffer, ('row', 'col'), split_axis=0, concat_axis=0, tiled...]
    pallas_call x1 -> x2, Pallas kernels: 65.7 us -> 86.5 us  [the longest x1 76.1 us: local(): pl.pallas_call(functools.partial(backward_kernel, rows, cols, block, scal...]
    ppermute x8 -> x4, starting transfers between devices: 30.5 us -> 11.2 us  [passed_along(): lax.ppermute(value, axis, [(source, source + steps) for source in range(i...]
    convert_element_type x2 -> x0, local copies, waits for them, and re-layouts: 13.1 us -> none  [the longest x1 11.9 us: local(): summed = summed_over_devices(stacked).astype(jnp.float32)]
    reshape x2 -> x0, local copies, waits for them, and re-layouts: 10.7 us -> none  [summed_over_devices(): halves = padded.reshape(devices, chunk, 2, width // 2).transpose(2, 0, 1, 3)]
    dot_general x5 -> x0, matrix products: 6.15 us -> none  [right_product(): lax.dot_general(first, second, (((1,), (1,)), ((), ())), preferred_elemen...]
  transfers between devices with their start and end apart: 12 -> 8, of which waited for: 3 -> 4; matrix products, arithmetic and copies ran while one was open for 26% -> 5% of each run, Pallas kernels for 22% -> 0%
where the time goes in v3:
time: 247 us; the launch traced here: 246 us
  waiting for transfers between devices  95.2 us (39%)
  Pallas kernels  86.5 us (35%)
  starting transfers between devices  27.6 us (11%)
  local copies, waits for them, and re-layouts  24.1 us (10%)
  matrix products  10.2 us (4%)
    all_to_all x4, waiting for transfers between devices, trade_slots(): lax.all_to_all(buffer, ('row', 'col'), split_axis=0, concat_axis=0, tiled...  95.2 us
    pallas_call x1, Pallas kernels, local(): pl.pallas_call(functools.partial(backward_kernel, rows, cols, block, scal...  76.1 us
    all_to_all x4, starting transfers between devices, trade_slots(): lax.all_to_all(buffer, ('row', 'col'), split_axis=0, concat_axis=0, tiled...  16.4 us
    unnamed x62, local copies, waits for them, and re-layouts  14.9 us
    ppermute x4, starting transfers between devices, passed_along(): lax.ppermute(value, axis, [(source, source + steps) for source in range(i...  11.2 us
    pallas_call x1, Pallas kernels, local(): pl.pallas_call(functools.partial(forward_kernel, block), out_shape=(shape...  10.5 us
    dot_general x6, matrix products, product(): return jnp.dot(first, second, preferred_element_type=jnp.float32)  5.18 us
    dot_general x3, matrix products, left_product(): lax.dot_general(first, second, (((0,), (0,)), ((), ())), preferred_elemen...  4.98 us
  transfers between devices with their start and end apart: 8, of which 4 were waited for; matrix products, arithmetic and copies ran while one was open for 5% of the time, Pallas kernels for 0%

profile of v3, /device:TPU:0, one launch (start us, length us, event | category | flops | bytes accessed | tf_op | source)
XLA Modules:
  0.0 246.5 jit_solution(17559958488984234120)
XLA Ops:
  0.6 0.0 copy-start
  0.6 0.0 copy-start.3
  0.7 0.0 copy-start.6
  0.7 0.0 copy-start.24
  0.7 0.9 eq.56
  1.5 1.3 convolution_convert_fusion.2
  2.9 1.3 collective-permute-start.3
  4.2 3.0 %collective-permute-start.2 = (bf16[32,512]{1,0:T(8,128)(2,1)S(1)}, bf16[32,512]{1,0:T(8,128)(2,1)S(1)}, u32[]{:S(2)}, u32[]{:S(2)}) collective-permute-start(bf16[32,512]{1,0:T(8,128)(2,1)S(1)} %get-tuple-element.36), channel_id=1, source_target_pairs={{0,1},{1,2},{2,3},{3,4},{4,5},{5,6},{6,7},{8,9},{9,10},{10,11},{11... | collective-permute-start | bytes 98312 | tf_op jit(solution)/shard_map/ppermute | solution.py:15
  7.2 1.3 collective-permute-start.1
  8.5 5.6 %collective-permute-start = (bf16[32,512]{1,0:T(8,128)(2,1)S(1)}, bf16[32,512]{1,0:T(8,128)(2,1)S(1)}, u32[]{:S(2)}, u32[]{:S(2)}) collective-permute-start(bf16[32,512]{1,0:T(8,128)(2,1)S(1)} %get-tuple-element.38), channel_id=1, source_target_pairs={{0,8},{8,16},{16,24},{1,9},{9,17},{17,25},{2,10},{10,18},{18,26},{... | collective-permute-start | bytes 98312 | tf_op jit(solution)/shard_map/ppermute | solution.py:15
  14.1 1.0 fusion.6
  15.1 0.7 convert_add_fusion
  15.8 1.1 copy.26.target_column
  16.9 0.0 copy-start.1
  16.9 0.4 copy.25.source_column
  17.3 0.0 collective-permute-done
  17.3 0.0 collective-permute-done.1
  17.3 0.0 collective-permute-done.2
  17.3 0.0 collective-permute-done.3
  17.3 0.0 copy-start.7
  17.4 0.0 copy-done.3
  17.4 0.0 copy-done.6
  17.4 0.0 copy-start.8
  17.4 1.3 copy-done.8
  18.6 1.0 copy-done.9
  19.7 1.0 copy-done.10
  20.7 1.0 copy-done.11
  21.8 1.0 copy-done.12
  22.8 10.5 %shard_map.188 = (bf16[2048,512]{1,0:T(8,128)(2,1)S(1)}, bf16[2048,512]{1,0:T(8,128)(2,1)S(1)}, bf16[2048,512]{1,0:T(8,128)(2,1)}, bf16[512,512]{1,0:T(8,128)(2,...) custom-call(bf16[512,512]{1,0:T(8,128)(2,1)S(1)} %copy-done.3, ...), custom_call_target="tpu_custom_call" | custom-call | flops 6442450944 | bytes 16777216 | tf_op jit(solution)/shard_map/pallas_call | solution.py:524
  33.3 0.0 copy-done.7
  33.3 1.0 copy-done.2
  34.2 0.8 copy-done.4
  35.0 1.4 copy-done.13
  36.4 1.3 copy-done.14
  37.7 1.0 copy-done.15
  38.7 0.8 copy-done.16
  39.5 0.8 copy-done.17
  40.3 5.4 %all-to-all-start = ((bf16[32,32,512]{2,1,0:T(8,128)(2,1)}), bf16[32,32,512]{2,1,0:T(8,128)(2,1)S(1)}, u32[]{:S(2)}, u32[]{:S(2)}) async-start(bf16[32,32,512]{2,1,0:T(8,128)(2,1)} %bitcast.24), calls=%async_computation | async-start | bytes 2097152 | tf_op jit(solution)/shard_map/all_to_all | solution.py:57
  45.7 0.0 copy-start.26
  45.7 1.8 fusion.2
  47.5 24.4 %all-to-all-done = bf16[32,32,512]{2,1,0:T(8,128)(2,1)S(1)} async-done(((bf16[32,32,512]{2,1,0:T(8,128)(2,1)}), bf16[32,32,512]{2,1,0:T(8,128)(2,1)S(1)}, u32[]{:S(2)}, u32[]{:S(2)}) %all-to-all-start) | async-done | bytes 1048608 | tf_op jit(solution)/shard_map/all_to_all | solution.py:57
  71.9 3.6 %all-to-all-start.2 = ((bf16[32,32,512]{2,1,0:T(8,128)(2,1)}), bf16[32,32,512]{2,1,0:T(8,128)(2,1)S(1)}, u32[]{:S(2)}, u32[]{:S(2)}) async-start(bf16[32,32,512]{2,1,0:T(8,128)(2,1)} %bitcast.34), calls=%async_computation.2 | async-start | bytes 2097152 | tf_op jit(solution)/shard_map/all_to_all | solution.py:57
  75.6 0.1 convert_reduce_fusion
  75.7 0.3 fusion.4.coarse
  76.0 0.2 fusion.23
  76.3 1.5 convolution_convert_fusion.1
  77.7 24.0 %all-to-all-done.2 = bf16[32,32,512]{2,1,0:T(8,128)(2,1)S(1)} async-done(((bf16[32,32,512]{2,1,0:T(8,128)(2,1)}), bf16[32,32,512]{2,1,0:T(8,128)(2,1)S(1)}, u32[]{:S(2)}, u32[]{:S(2)}) %all-to-all-start.2) | async-done | bytes 1048608 | tf_op jit(solution)/shard_map/all_to_all | solution.py:57
  101.8 3.6 %all-to-all-start.1 = ((bf16[32,32,512]{2,1,0:T(8,128)(2,1)}), bf16[32,32,512]{2,1,0:T(8,128)(2,1)S(1)}, u32[]{:S(2)}, u32[]{:S(2)}) async-start(bf16[32,32,512]{2,1,0:T(8,128)(2,1)} %bitcast.36), calls=%async_computation.1 | async-start | bytes 2097152 | tf_op jit(solution)/shard_map/all_to_all | solution.py:57
  105.4 0.3 fusion.5.grad_coarse
  105.7 0.0 copy-start.25
  105.8 1.7 convolution_convert_fusion
  107.5 24.2 %all-to-all-done.1 = bf16[32,32,512]{2,1,0:T(8,128)(2,1)S(1)} async-done(((bf16[32,32,512]{2,1,0:T(8,128)(2,1)}), bf16[32,32,512]{2,1,0:T(8,128)(2,1)S(1)}, u32[]{:S(2)}, u32[]{:S(2)}) %all-to-all-start.1) | async-done | bytes 1048608 | tf_op jit(solution)/shard_map/all_to_all | solution.py:57
  131.7 3.8 %all-to-all-start.3 = ((bf16[32,32,512]{2,1,0:T(8,128)(2,1)}), bf16[32,32,512]{2,1,0:T(8,128)(2,1)S(1)}, u32[]{:S(2)}, u32[]{:S(2)}) async-start(bf16[32,32,512]{2,1,0:T(8,128)(2,1)} %bitcast.35), calls=%async_computation.3 | async-start | bytes 2097152 | tf_op jit(solution)/shard_map/all_to_all | solution.py:57
  135.5 0.7 broadcast_in_dim_reshape_squeeze.4.list_row
  136.1 0.8 copy.27.slot_column
  137.0 2.0 fusion.1
  139.0 22.6 %all-to-all-done.3 = bf16[32,32,512]{2,1,0:T(8,128)(2,1)S(1)} async-done(((bf16[32,32,512]{2,1,0:T(8,128)(2,1)}), bf16[32,32,512]{2,1,0:T(8,128)(2,1)S(1)}, u32[]{:S(2)}, u32[]{:S(2)}) %all-to-all-start.3) | async-done | bytes 1048608 | tf_op jit(solution)/shard_map/all_to_all | solution.py:57
  161.5 1.0 copy-done.21
  162.5 76.1 %shard_map.189 = (f32[512,512]{1,0:T(8,128)}, bf16[2048,512]{1,0:T(8,128)(2,1)}, bf16[1536,512]{1,0:T(8,128)(2,1)}) custom-call(bf16[512,512]{1,0:T(8,128)(2,1)} %nodes.3, bf16[128,512]{1,0:T(8,128)(2,1)} %copy-done.7, bf16[512,512]{1,0:T(8,128)(2,1)} %cotangent.1, bf16[1024,512]{1,0:T(8,128)(2,1)} %bitcast.30, s32[512,1]{1,0:T(8,128)} %copy.27.slot_column, ...), custom_call_target="tpu_custom_call" | custom-call | flops 8589934592 | bytes 25165824 | tf_op jit(solution)/shard_map/pallas_call | solution.py:571
  238.6 3.0 %slice.51 = f32[1024,512]{1,0:T(8,128)} slice(bf16[2048,512]{1,0:T(8,128)(2,1)} %get-tuple-element.29), slice={[1024:2048], [0:512]} | slice | bytes 4194304 | tf_op jit(solution)/shard_map/slice | solution.py:631
  241.6 2.5 %fusion.20 = (f32[512,512]{1,0:T(8,128)}, f32[512,512]{1,0:T(8,128)}, f32[512,512]{1,0:T(8,128)}, f32[512,512]{1,0:T(8,128)}, f32[512,512]{1,0:T(8,128)}) fusion(bf16[2048,512]{1,0:T(8,128)(2,1)S(1)} %copy-done.18, bf16[1536,512]{1,0:T(8,128)(2,1)S(1)} %copy-done.19), kind=kLoop, calls=%fused_computation.42 | loop fusion | bytes 10485760 | tf_op jit(solution)/shard_map/slice | solution.py:633
  244.1 1.0 add_convert_fusion
  245.1 0.4 copy-done.20
  245.5 1.0 copy.33
  (38 shorter events, 0.1 us)
Async XLA Ops:
  0.6 75.4 %copy-start = (bf16[512,512]{1,0:T(8,128)(2,1)S(1)}, bf16[512,512]{1,0:T(8,128)(2,1)}, u32[]{:S(2)}) copy-start(bf16[512,512]{1,0:T(8,128)(2,1)} %param.25) | copy-start | bytes 1572868
  0.6 16.7 %copy-start.3 = (bf16[512,512]{1,0:T(8,128)(2,1)S(1)}, bf16[512,512]{1,0:T(8,128)(2,1)}, u32[]{:S(2)}) copy-start(bf16[512,512]{1,0:T(8,128)(2,1)} %nodes.3) | copy-start | bytes 1572868
  0.7 16.7 %copy-start.6 = (s32[2048]{0:T(1024)S(1)}, s32[2048]{0:T(1024)}, u32[]{:S(2)}) copy-start(s32[2048]{0:T(1024)} %param.16) | copy-start | bytes 24580
  0.7 16.2 %copy-start.24 = (s32[2048]{0:T(1024)S(1)}, s32[2048]{0:T(1024)}, u32[]{:S(2)}) copy-start(s32[2048]{0:T(1024)} %param.15) | copy-start | bytes 24580
  2.9 14.5 %collective-permute-start.3 = (bf16[32,512]{1,0:T(8,128)(2,1)S(1)}, bf16[32,512]{1,0:T(8,128)(2,1)S(1)}, u32[]{:S(2)}, u32[]{:S(2)}) collective-permute-start(bf16[32,512]{1,0:T(8,128)(2,1)S(1)} %get-tuple-element.35), channel_id=1, source_target_pairs={{1,0},{2,1},{3,2},{4,3},{5,4},{6,5},{7,6},{9,8},{10,9},{11,10},{12... | collective-permute-start | bytes 98312 | tf_op jit(solution)/shard_map/ppermute | solution.py:15
  4.2 13.1 %collective-permute-start.2 = (bf16[32,512]{1,0:T(8,128)(2,1)S(1)}, bf16[32,512]{1,0:T(8,128)(2,1)S(1)}, u32[]{:S(2)}, u32[]{:S(2)}) collective-permute-start(bf16[32,512]{1,0:T(8,128)(2,1)S(1)} %get-tuple-element.36), channel_id=1, source_target_pairs={{0,1},{1,2},{2,3},{3,4},{4,5},{5,6},{6,7},{8,9},{9,10},{10,11},{11... | collective-permute-start | bytes 98312 | tf_op jit(solution)/shard_map/ppermute | solution.py:15
  7.2 10.1 %collective-permute-start.1 = (bf16[32,512]{1,0:T(8,128)(2,1)S(1)}, bf16[32,512]{1,0:T(8,128)(2,1)S(1)}, u32[]{:S(2)}, u32[]{:S(2)}) collective-permute-start(bf16[32,512]{1,0:T(8,128)(2,1)S(1)} %get-tuple-element.37), channel_id=1, source_target_pairs={{8,0},{16,8},{24,16},{9,1},{17,9},{25,17},{10,2},{18,10},{26,18},{... | collective-permute-start | bytes 98312 | tf_op jit(solution)/shard_map/ppermute | solution.py:15
  8.5 8.7 %collective-permute-start = (bf16[32,512]{1,0:T(8,128)(2,1)S(1)}, bf16[32,512]{1,0:T(8,128)(2,1)S(1)}, u32[]{:S(2)}, u32[]{:S(2)}) collective-permute-start(bf16[32,512]{1,0:T(8,128)(2,1)S(1)} %get-tuple-element.38), channel_id=1, source_target_pairs={{0,8},{8,16},{16,24},{1,9},{9,17},{17,25},{2,10},{10,18},{18,26},{... | collective-permute-start | bytes 98312 | tf_op jit(solution)/shard_map/ppermute | solution.py:15
  16.9 16.4 %copy-start.1 = (s32[2048,1]{1,0:T(8,128)}, s32[2048,1]{1,0:T(8,128)S(1)}, u32[]{:S(2)}) copy-start(s32[2048,1]{1,0:T(8,128)S(1)} %copy.26.target_column) | copy-start | bytes 24580
  17.3 15.9 %copy-start.7 = (bf16[128,512]{1,0:T(8,128)(2,1)}, bf16[128,512]{1,0:T(8,128)(2,1)S(1)}, u32[]{:S(2)}) copy-start(bf16[128,512]{1,0:T(8,128)(2,1)S(1)} %constant_dynamic-update-slice_fusion.halo) | copy-start | bytes 393220
  17.4 1.3 copy-start.8
  18.6 1.0 copy-start.9
  19.7 1.0 copy-start.10
  20.7 1.0 copy-start.11
  21.8 1.0 copy-start.12
  33.3 1.0 copy-start.2
  34.2 0.8 copy-start.4
  35.0 1.4 copy-start.13
  36.4 1.3 copy-start.14
  37.7 1.0 copy-start.15
  38.7 0.8 copy-start.16
  39.5 0.8 copy-start.17
  40.3 5.4 %copy-start.27 = (bf16[512,512]{1,0:T(8,128)(2,1)S(1)}, bf16[512,512]{1,0:T(8,128)(2,1)}, u32[]{:S(2)}) copy-start(bf16[512,512]{1,0:T(8,128)(2,1)} %cotangent.1) | copy-start | bytes 1572868
  40.3 31.6 %all-to-all-start = ((bf16[32,32,512]{2,1,0:T(8,128)(2,1)}), bf16[32,32,512]{2,1,0:T(8,128)(2,1)S(1)}, u32[]{:S(2)}, u32[]{:S(2)}) async-start(bf16[32,32,512]{2,1,0:T(8,128)(2,1)} %bitcast.24), calls=%async_computation | async-start | bytes 2097152 | tf_op jit(solution)/shard_map/all_to_all | solution.py:57
  45.7 29.9 %copy-start.26 = (s32[1,1024]{1,0:T(1,128)S(1)}, s32[1,1024]{1,0:T(1,128)}, u32[]{:S(2)}) copy-start(s32[1,1024]{1,0:T(1,128)} %param.19) | copy-start | bytes 12292
  71.9 29.9 %all-to-all-start.2 = ((bf16[32,32,512]{2,1,0:T(8,128)(2,1)}), bf16[32,32,512]{2,1,0:T(8,128)(2,1)S(1)}, u32[]{:S(2)}, u32[]{:S(2)}) async-start(bf16[32,32,512]{2,1,0:T(8,128)(2,1)} %bitcast.34), calls=%async_computation.2 | async-start | bytes 2097152 | tf_op jit(solution)/shard_map/all_to_all | solution.py:57
  76.0 25.8 %copy-start.23 = (bf16[128,512]{1,0:T(8,128)(2,1)}, bf16[128,512]{1,0:T(8,128)(2,1)S(1)}, u32[]{:S(2)}) copy-start(bf16[128,512]{1,0:T(8,128)(2,1)S(1)} %fusion.4.coarse) | copy-start | bytes 393220
  101.8 29.9 %all-to-all-start.1 = ((bf16[32,32,512]{2,1,0:T(8,128)(2,1)}), bf16[32,32,512]{2,1,0:T(8,128)(2,1)S(1)}, u32[]{:S(2)}, u32[]{:S(2)}) async-start(bf16[32,32,512]{2,1,0:T(8,128)(2,1)} %bitcast.36), calls=%async_computation.1 | async-start | bytes 2097152 | tf_op jit(solution)/shard_map/all_to_all | solution.py:57
  105.7 33.2 %copy-start.28 = (bf16[128,512]{1,0:T(8,128)(2,1)}, bf16[128,512]{1,0:T(8,128)(2,1)S(1)}, u32[]{:S(2)}) copy-start(bf16[128,512]{1,0:T(8,128)(2,1)S(1)} %fusion.5.grad_coarse) | copy-start | bytes 393220
  105.7 29.7 %copy-start.25 = (s32[1,4,32]{2,1,0:T(4,128)S(1)}, s32[1,4,32]{2,1,0:T(4,128)}, u32[]{:S(2)}) copy-start(s32[1,4,32]{2,1,0:T(4,128)} %param.17) | copy-start | bytes 1540
  131.7 5.3 %copy-start.22 = (bf16[32,32,512]{2,1,0:T(8,128)(2,1)}, bf16[32,32,512]{2,1,0:T(8,128)(2,1)S(1)}, u32[]{:S(2)}) copy-start(bf16[32,32,512]{2,1,0:T(8,128)(2,1)S(1)} %all-to-all-done.1) | copy-start | bytes 3145732
  131.7 29.9 %all-to-all-start.3 = ((bf16[32,32,512]{2,1,0:T(8,128)(2,1)}), bf16[32,32,512]{2,1,0:T(8,128)(2,1)S(1)}, u32[]{:S(2)}, u32[]{:S(2)}) async-start(bf16[32,32,512]{2,1,0:T(8,128)(2,1)} %bitcast.35), calls=%async_computation.3 | async-start | bytes 2097152 | tf_op jit(solution)/shard_map/all_to_all | solution.py:57
  161.5 1.0 copy-start.21
  238.6 3.0 %copy-start.18 = (bf16[2048,512]{1,0:T(8,128)(2,1)S(1)}, bf16[2048,512]{1,0:T(8,128)(2,1)}, u32[]{:S(2)}) copy-start(bf16[2048,512]{1,0:T(8,128)(2,1)} %get-tuple-element.29) | copy-start | bytes 6291460
  238.6 3.0 %copy-start.19 = (bf16[1536,512]{1,0:T(8,128)(2,1)S(1)}, bf16[1536,512]{1,0:T(8,128)(2,1)}, u32[]{:S(2)}) copy-start(bf16[1536,512]{1,0:T(8,128)(2,1)} %get-tuple-element.28) | copy-start | bytes 4718596
  241.6 2.5 %copy-start.5 = (bf16[512,512]{1,0:T(8,128)(2,1)S(1)}, bf16[512,512]{1,0:T(8,128)(2,1)}, u32[]{:S(2)}) copy-start(bf16[512,512]{1,0:T(8,128)(2,1)} %copy-done.4) | copy-start | bytes 1572868
  244.1 1.4 copy-start.20

commit v4 on v3

--- a/solution.py
+++ b/solution.py
@@ -213,10 +213,89 @@
     return sigma * (1.0 + value * (1.0 - sigma))
 
 
+class Trade:
+    def __init__(self, rows, cols, away, home, send, recv):
+        self.devices, self.cols = rows * cols, cols
+        self.away, self.home, self.send, self.recv = away, home, send, recv
+        self.me = lax.axis_index("row") * cols + lax.axis_index("col")
+
+    def place(self, ahead):
+        peer = lax.rem(self.me + ahead, jnp.int32(self.devices))
+        return peer, (lax.div(peer, jnp.int32(self.cols)), lax.rem(peer, jnp.int32(self.cols)))
+
+    def copy(self, ahead):
+        peer, position = self.place(ahead)
+        return pltpu.make_async_remote_copy(
+            src_ref=self.away.at[peer],
+            dst_ref=self.home.at[self.me],
+            send_sem=self.send.at[ahead],
+            recv_sem=self.recv.at[ahead],
+            device_id=position,
+            device_id_type=pl.DeviceIdType.MESH,
+        )
+
+    def greet(self, barrier):
+        def signal(ahead, carry):
+            pl.semaphore_signal(
+                barrier,
+                inc=1,
+                device_id=self.place(ahead)[1],
+                device_id_type=pl.DeviceIdType.MESH,
+            )
+            return carry
+
+        lax.fori_loop(1, self.devices, signal, 0)
+
+    def start(self):
+        def begin(ahead, carry):
+            self.copy(ahead).start()
+            return carry
+
+        lax.fori_loop(1, self.devices, begin, 0)
+        self.home[self.me] = self.away[self.me]
+
+    def finish(self):
+        def end(ahead, carry):
+            self.copy(ahead).wait()
+            return carry
+
+        lax.fori_loop(1, self.devices, end, 0)
+
+    def rows(self):
+        return self.home[...].reshape(self.devices * self.home.shape[1], self.home.shape[2])
+
+
+def fill_slots(slot_row, values, slots):
+    devices, capacity, width = slots.shape
+    group = max(1, 512 // capacity)
+    for start in range(0, devices, group):
+        count = min(group, devices - start)
+        spread = lax.broadcasted_iota(jnp.int32, (count * capacity, slot_row.shape[1]), 0)
+        hot = jnp.where(spread + start * capacity == slot_row, 1.0, 0.0).astype(jnp.bfloat16)
+        slots[start : start + count] = low(product(hot, values)).reshape(count, capacity, width)
+
+
+def ring_neighbours(rows, cols):
+    row, col = lax.axis_index("row"), lax.axis_index("col")
+    return [
+        (lax.rem(row + rows - 1, jnp.int32(rows)), col),
+        (lax.rem(row + 1, jnp.int32(rows)), col),
+        (row, lax.rem(col + cols - 1, jnp.int32(cols))),
+        (row, lax.rem(col + 1, jnp.int32(cols))),
+    ]
+
+
 def forward_kernel(
+    rows,
+    cols,
     block,
     nodes,
-    halo,
+    cotangent,
+    list_column,
+    slot_column,
+    table_row,
+    table_column,
+    coarse_weight,
     source_column,
     target_column,
     target_row,
@@ -233,16 +312,70 @@
     node_linear,
     node_hidden,
     refined,
-    slots,
+    halo,
+    share_rows,
+    coarse,
+    grad_coarse,
+    update_slots,
     sides,
     sums,
+    picked,
+    landed,
+    first_away,
+    first_home,
+    second_away,
+    second_home,
+    third_away,
+    third_home,
+    first_send,
+    first_recv,
+    second_send,
+    second_recv,
+    third_send,
+    third_recv,
+    halo_send,
+    halo_recv,
 ):
+    first = Trade(rows, cols, first_away, first_home, first_send, first_recv)
+    second = Trade(rows, cols, second_away, second_home, second_send, second_recv)
+    third = Trade(rows, cols, third_away, third_home, third_send, third_recv)
+    barrier = pltpu.get_barrier_semaphore()
+    first.greet(barrier)
     count_rows, width = nodes.shape
     own = nodes[...]
     extra = halo.shape[0]
+    each = extra // 4
+    picked[...] = low(product(hot_rows(list_column[...], count_rows), own))
+    fill_slots(slot_row[...], cotangent[...], first_away)
+    pl.semaphore_wait(barrier, rows * cols - 1)
+    neighbours = ring_neighbours(rows, cols)
+    row, col = lax.axis_index("row"), lax.axis_index("col")
+    sends = []
+    for number, target in enumerate((1, 0, 3, 2)):
+        here = pl.ds(number * each, each)
+        sends.append(
+            pltpu.make_async_remote_copy(
+                src_ref=picked.at[here],
+                dst_ref=landed.at[here],
+                send_sem=halo_send.at[number],
+                recv_sem=halo_recv.at[number],
+                device_id=neighbours[target],
+                device_id_type=pl.DeviceIdType.MESH,
+            )
+        )
+    for copy in sends:
+        copy.start()
+    first.start()
     sides[0:count_rows, :] = low(product(own, source_weight[...]))
+    sides[count_rows + extra :, :] = low(product(own, target_weight[...]))
+    for copy in sends:
+        copy.wait()
+    inside = [row > 0, row + 1 < rows, col > 0, col + 1 < cols]
+    for number in range(4):
+        here = pl.ds(number * each, each)
+        keep = jnp.where(inside[number], 1.0, 0.0).astype(jnp.bfloat16)
+        halo[here, :] = landed[here, :] * keep
     sides[count_rows : count_rows + extra, :] = low(product(halo[...], source_weight[...]))
-    sides[count_rows + extra :, :] = low(product(own, target_weight[...]))
     sums[...] = jnp.zeros_like(sums)
 
     @pl.loop(0, edge_linear.shape[0] // block)
@@ -269,12 +402,27 @@
     node_hidden[...] = hidden
     result = low(own.astype(jnp.float32) + product(hidden, outer_weight[...]))
     refined[...] = result
-    places = slots.shape[0]
-    step = count_rows
-    for start in range(0, places, step):
-        spread = lax.broadcasted_iota(jnp.int32, (step, count_rows), 0) + start
-        hot = jnp.where(spread == slot_row[...], 1.0, 0.0).astype(jnp.bfloat16)
-        slots[start : start + step, :] = low(product(hot, result))
+    fill_slots(slot_row[...], result, second_away)
+    second.start()
+    member = hot_columns(table_row[...], count_rows // 4)
+    count = jnp.maximum(jnp.sum(member.astype(jnp.float32), axis=1, keepdims=True), 1.0)
+    first.finish()
+    pooled_cotangent = product(member, first.rows())
+    second.finish()
+    pooled = low(product(member, second.rows()) / count)
+    coarse[...] = pooled
+    linear = product(pooled, coarse_weight[...])
+    gradient = low(pooled_cotangent * slope(linear))
+    grad_coarse[...] = gradient
+    share = low(right_product(gradient, coarse_weight[...]) / count)
+    spread = hot_rows(table_column[...], count_rows // 4)
+    third_away[...] = low(product(spread, share)).reshape(third_away.shape)
+    third.start()
+    update = low(linear * sigmoid(linear))
+    update_slots[...] = low(product(spread, update)).reshape(update_slots.shape)
+    third.finish()
+    places = third_home.shape[0] * third_home.shape[1]
+    share_rows[...] = product(hot_rows(slot_column[...], places), third.rows())
 
 
 def pack(flat, own):
@@ -313,7 +461,9 @@
     nodes,
     halo,
     cotangent,
-    shares,
+    share_rows,
+    refined,
+    update_slots,
     slot_column,
     target_column,
     source_row,
@@ -333,6 +483,7 @@
     node_linear,
     node_hidden,
     node_gradient,
+    updated,
     early_sums,
     late_sums,
     early_flat,
@@ -349,6 +500,10 @@
     edge_sums,
     blocks,
     landed,
+    update_away,
+    update_home,
+    update_send,
+    update_recv,
     early_send,
     early_recv,
     late_send,
@@ -359,25 +514,16 @@
     early = Summation(rows, cols, early_own, early_land, early_out, early_send, early_recv)
     late = Summation(rows, cols, late_own, late_land, late_out, late_send, late_recv)
     row, col = early.row, early.col
-    neighbours = [
-        (lax.rem(row + rows - 1, jnp.int32(rows)), col),
-        (lax.rem(row + 1, jnp.int32(rows)), col),
-        (row, lax.rem(col + cols - 1, jnp.int32(cols))),
-        (row, lax.rem(col + 1, jnp.int32(cols))),
-    ]
+    neighbours = ring_neighbours(rows, cols)
+    trade = Trade(rows, cols, update_away, update_home, update_send, update_recv)
     barrier = pltpu.get_barrier_semaphore()
-    peers = [(row, early.across(bit)) for bit in range(early.bits)]
-    peers += [(early.along(ahead), col) for ahead in range(1, rows)]
-    peers += neighbours[2:]
-    for peer in peers:
-        pl.semaphore_signal(barrier, inc=1, device_id=peer, device_id_type=pl.DeviceIdType.MESH)
+    trade.greet(barrier)
 
     count_rows, width = nodes.shape
     extra = halo.shape[0]
     each = extra // 4
     own = nodes[...]
-    share_rows = product(hot_rows(slot_column[...], shares.shape[0]), shares[...])
-    grad_refined = cotangent[...].astype(jnp.float32) + share_rows
+    grad_refined = cotangent[...].astype(jnp.float32) + share_rows[...]
     refined_low = low(grad_refined)
     early_flat[0:width, :] = low(scale * left_product(coarse[...], grad_coarse[...]))
     early_flat[width : 2 * width, :] = low(scale * left_product(node_hidden[...], refined_low))
@@ -385,8 +531,10 @@
     early_flat[2 * width : 3 * width, :] = low(scale * left_product(own, grad_hidden))
     early_flat[3 * width : 4 * width, :] = low(scale * left_product(aggregate[...], grad_hidden))
     pack(early_flat, early_own)
-    pl.semaphore_wait(barrier, len(peers))
+    update_away[...] = update_slots[...]
+    pl.semaphore_wait(barrier, rows * cols - 1)
     early.begin()
+    trade.start()
     grad_aggregate[...] = low(right_product(grad_hidden, inner_weight[width:, :]))
     node_gradient[...] = grad_refined + right_product(grad_hidden, inner_weight[0:width, :])
     source_sums[...] = jnp.zeros_like(source_sums)
@@ -450,6 +598,11 @@
         keep = jnp.where(inside[number], 1.0, 0.0).astype(jnp.bfloat16)
         landed[here, :] = landed[here, :] * keep
     node_gradient[...] += product(hot_columns(list_row[...], count_rows), landed[...])
+    trade.finish()
+    places = update_home.shape[0] * update_home.shape[1]
+    updated[...] = low(
+        refined[...].astype(jnp.float32) + product(hot_rows(slot_column[...], places), trade.rows())
+    )
     for step in range(late.steps):
         if done + step < early.steps:
             early.advance(done + step)
@@ -483,28 +636,16 @@
     coarse_rows = count_rows // 4
     scale = 1.0 / math.sqrt(count_rows * devices)
     all_lists = lists.reshape(-1)
+    room = max(capacity, 16)
+    table = jnp.pad(
+        table.reshape(devices, capacity), ((0, 0), (0, room - capacity)), constant_values=-1
+    ).reshape(devices * room)
     owner_hot = one_hot(pool_owner, devices)
     positions = jnp.arange(count_rows, dtype=jnp.int32)
     lower = (positions[:, None] > positions[None, :]).astype(jnp.bfloat16)
     rank = jnp.sum(product(lower, owner_hot) * owner_hot, axis=1).astype(jnp.int32)
-    slot = pool_owner * capacity + rank
-    slot_hot = one_hot(slot, devices * capacity)
-    member = (jnp.arange(coarse_rows, dtype=jnp.int32)[:, None] == table[None, :]).astype(
-        jnp.bfloat16
-    )
-    count = jnp.maximum(jnp.sum(member, axis=1, dtype=jnp.float32), 1.0)[:, None]
-
-    def toward_owners(values):
-        return product(member, trade_slots(low(left_product(slot_hot, values))))
-
-    def toward_sources(values):
-        return product(slot_hot, trade_slots(low(left_product(member, values))))
-
-    list_hot = one_hot(all_lists, count_rows)
-    picked = low(product(list_hot, nodes)).reshape(4, halo_rows, width)
-    received = trade_halo([picked[number] for number in range(4)], 1)
-    pooled_cotangent = toward_owners(cotangent)
-    halo = jnp.concatenate(received, axis=0)
+    slot = pool_owner * room + rank
+    rows, cols = lax.axis_size("row"), lax.axis_size("col")
     edges = edge_source.shape[0]
     block = math.gcd(512, edges)
     source_column, target_column = edge_source[:, None], edge_target[:, None]
@@ -520,9 +661,13 @@
         node_linear,
         node_hidden,
         refined,
-        refined_slots,
+        halo,
+        share_rows,
+        coarse,
+        grad_coarse,
+        update_slots,
     ) = pl.pallas_call(
-        functools.partial(forward_kernel, block),
+        functools.partial(forward_kernel, rows, cols, block),
         out_shape=(
             shaped((edges, width), jnp.bfloat16),
             shaped((edges, width), jnp.bfloat16),
@@ -531,21 +676,36 @@
             shaped((count_rows, width), jnp.float32),
             shaped((count_rows, width), jnp.bfloat16),
             shaped((count_rows, width), jnp.bfloat16),
-            shaped((devices * capacity, width), jnp.bfloat16),
+            shaped((4 * halo_rows, width), jnp.bfloat16),
+            shaped((count_rows, width), jnp.float32),
+            shaped((coarse_rows, width), jnp.bfloat16),
+            shaped((coarse_rows, width), jnp.bfloat16),
+            shaped((devices, room, width), jnp.bfloat16),
         ),
-        in_specs=[whole] * 11,
-        out_specs=[whole] * 8,
+        in_specs=[whole] * 16,
+        out_specs=[whole] * 12,
         scratch_shapes=[
             pltpu.VMEM((2 * count_rows + 4 * halo_rows, width), jnp.bfloat16),
             pltpu.VMEM((count_rows, width), jnp.float32),
-        ],
-        compiler_params=pltpu.CompilerParams(vmem_limit_bytes=40 << 20),
+        ]
+        + [pltpu.VMEM((4 * halo_rows, width), jnp.bfloat16)] * 2
+        + [pltpu.VMEM((devices, room, width), jnp.bfloat16)] * 6
+        + [pltpu.SemaphoreType.DMA((devices,))] * 6
+        + [pltpu.SemaphoreType.DMA((4,))] * 2,
+        compiler_params=pltpu.CompilerParams(
+            collective_id=2, has_side_effects=True, vmem_limit_bytes=56 << 20
+        ),
         cost_estimate=pl.CostEstimate(
             flops=6 * edges * width * width * 2, bytes_accessed=16 << 20, transcendentals=0
         ),
     )(
         nodes,
-        halo,
+        cotangent,
+        all_lists[:, None],
+        slot[:, None],
+        table[None, :],
+        table[:, None],
+        coarse_weight,
         source_column,
         target_column,
         target_row,
@@ -556,27 +716,21 @@
         inner_weight,
         outer_weight,
     )
-    coarse = low(product(member, trade_slots(refined_slots)) / count)
-    coarse_linear = product(coarse, coarse_weight)
-    coarse_update = low(jax.nn.silu(coarse_linear))
-    grad_coarse = low(pooled_cotangent * silu_slope(coarse_linear))
-    coarse_share = low(right_product(grad_coarse, coarse_weight) / count)
-    shares = trade_slots(low(left_product(member, coarse_share)))
-    rows, cols = lax.axis_size("row"), lax.axis_size("col")
     semaphores = Summation.semaphores(rows, cols)
     heights = (4 * width, 3 * width)
     chunks = [-(-height // (16 * devices)) * 16 for height in heights]
     flats = [(devices * chunk, width) for chunk in chunks]
     cuts = [(2, devices, chunk, width // 2) for chunk in chunks]
-    node_gradient, early_sums, late_sums = pl.pallas_call(
+    node_gradient, updated, early_sums, late_sums = pl.pallas_call(
         functools.partial(backward_kernel, rows, cols, block, scale),
         out_shape=(
             shaped((count_rows, width), jnp.float32),
+            shaped((count_rows, width), jnp.bfloat16),
             shaped(flats[0], jnp.bfloat16),
             shaped(flats[1], jnp.bfloat16),
         ),
-        in_specs=[whole] * 22,
-        out_specs=[whole] * 3,
+        in_specs=[whole] * 24,
+        out_specs=[whole] * 4,
         scratch_shapes=[pltpu.VMEM(flat, jnp.bfloat16) for flat in flats]
         + [pltpu.VMEM(cuts[0], jnp.bfloat16)] * 3
         + [pltpu.VMEM(cuts[1], jnp.bfloat16)] * 3
@@ -588,6 +742,8 @@
             pltpu.VMEM((4 * halo_rows, width), jnp.bfloat16),
             pltpu.VMEM((4 * halo_rows, width), jnp.bfloat16),
         ]
+        + [pltpu.VMEM((devices, room, width), jnp.bfloat16)] * 2
+        + [pltpu.SemaphoreType.DMA((devices,))] * 2
         + [pltpu.SemaphoreType.DMA((2, semaphores))] * 4
         + [pltpu.SemaphoreType.DMA((4,))] * 2,
         compiler_params=pltpu.CompilerParams(
@@ -600,7 +756,9 @@
         nodes,
         halo,
         cotangent,
-        shares.reshape(devices * capacity, width),
+        share_rows,
+        refined,
+        update_slots,
         slot[:, None],
         target_column,
         source_row,
@@ -620,7 +778,6 @@
         node_linear,
         node_hidden,
     )
-    updated = low(refined.astype(jnp.float32) + toward_sources(coarse_update))
     early_sums, late_sums = early_sums.astype(jnp.float32), late_sums.astype(jnp.float32)
     return (
         updated,

time: 247 us -> 197 us (0.80)
  waiting for transfers between devices: 95.2 us -> 0 us
  Pallas kernels: 86.5 us -> 178 us
  starting transfers between devices: 27.6 us -> 0 us
  matrix products: 10.2 us -> 1.03 us
  local copies, waits for them, and re-layouts: 24.1 us -> 15.9 us
    all_to_all x4 -> x0, waiting for transfers between devices: 95.2 us -> none  [trade_slots(): lax.all_to_all(buffer, ('row', 'col'), split_axis=0, concat_axis=0, tiled...]
    pallas_call x1, Pallas kernels: 10.5 us -> 77.9 us  [local(): pl.pallas_call(functools.partial(forward_kernel, rows, cols, block), out_...]
    pallas_call x1, Pallas kernels: 76.1 us -> 100 us  [local(): pl.pallas_call(functools.partial(backward_kernel, rows, cols, block, scal...]
    all_to_all x4 -> x0, starting transfers between devices: 16.4 us -> none  [trade_slots(): lax.all_to_all(buffer, ('row', 'col'), split_axis=0, concat_axis=0, tiled...]
    unnamed x62 -> x14, local copies, waits for them, and re-layouts: 14.9 us -> 1.79 us
    ppermute x4 -> x0, starting transfers between devices: 11.2 us -> none  [passed_along(): lax.ppermute(value, axis, [(source, source + steps) for source in range(i...]
    dot_general x3 -> x0, matrix products: 4.98 us -> none  [left_product(): lax.dot_general(first, second, (((0,), (0,)), ((), ())), preferred_elemen...]
    dot_general x6 -> x1, matrix products: 5.18 us -> 1.03 us  [product(): return jnp.dot(first, second, preferred_element_type=jnp.float32)]
  transfers between devices with their start and end apart: 8 -> 0, of which waited for: 4 -> 0; matrix products, arithmetic and copies ran while one was open for 5% -> 0% of each run, Pallas kernels for 0% -> 0%
where the time goes in v4:
time: 197 us; the launch traced here: 196 us
  Pallas kernels  178 us (90%)
  local copies, waits for them, and re-layouts  15.9 us (8%)
    pallas_call x1, Pallas kernels, local(): pl.pallas_call(functools.partial(backward_kernel, rows, cols, block, scal...  100 us
    pallas_call x1, Pallas kernels, local(): pl.pallas_call(functools.partial(forward_kernel, rows, cols, block), out_...  77.9 us

profile of v4, /device:TPU:0, one launch (start us, length us, event | category | flops | bytes accessed | tf_op | source)
XLA Modules:
  0.0 196.3 jit_solution(6260840266205903908)
XLA Ops:
  0.6 0.0 copy-start.4
  0.6 1.3 broadcast_in_dim_reshape_squeeze.7.list_row
  1.9 1.0 fusion
  3.0 0.7 convert_add_fusion
  3.6 0.0 copy-start.5
  3.6 1.4 broadcast_in_dim_reshape_squeeze.8.list_column
  5.1 0.9 copy.23.slot_column
  5.9 1.7 copy.24.table_column
  7.6 2.0 %copy.26.target_column = s32[2048,1]{1,0:T(8,128)} copy(s32[2048,1]{0,1:T(1,128)} %bitcast.9) | data formatting | bytes 16384 | tf_op jit(solution)/shard_map/broadcast_in_dim | solution.py:651
  9.7 0.0 copy-done.4
  9.7 1.3 copy.25.source_column
  11.0 0.0 copy-done.5
  11.0 77.9 %shard_map.188 = (bf16[2048,512]{1,0:T(8,128)(2,1)}, bf16[2048,512]{1,0:T(8,128)(2,1)}, bf16[2048,512]{1,0:T(8,128)(2,1)}, bf16[512,512]{1,0:T(8,128)(2,1)}, f32...) custom-call(bf16[512,512]{1,0:T(8,128)(2,1)} %nodes.3, ...), custom_call_target="tpu_custom_call" | custom-call | flops 6442450944 | bytes 16777216 | tf_op jit(solution)/shard_map/pallas_call | solution.py:669
  88.9 100.1 %shard_map.189 = (f32[512,512]{1,0:T(8,128)}, bf16[512,512]{1,0:T(8,128)(2,1)}, bf16[2048,512]{1,0:T(8,128)(2,1)}, bf16[1536,512]{1,0:T(8,128)(2,1)}) custom-call(bf16[512,512]{1,0:T(8,128)(2,1)} %nodes.3, bf16[128,512]{1,0:T(8,128)(2,1)} %get-tuple-element.24.halo, bf16[512,512]{1,0:T(8,128)(2,1)} %cotangent.3, f32[512,512]{1,0:T(8,128)} %get-tuple-element.25.share_rows, ...), custom_call_target="tpu_custom_call" | custom-call | flops 8589934592 | bytes 25165824 | tf_op jit(solution)/shard_map/pallas_call | solution.py:724
  189.0 0.0 copy-start
  189.1 0.0 copy-start.1
  189.1 3.0 %slice.27 = f32[1024,512]{1,0:T(8,128)} slice(bf16[2048,512]{1,0:T(8,128)(2,1)} %get-tuple-element.39), slice={[1024:2048], [0:512]} | slice | bytes 4194304 | tf_op jit(solution)/shard_map/slice | solution.py:788
  192.0 0.0 copy-done
  192.1 0.0 copy-done.1
  192.1 0.0 copy-start.3
  192.1 0.0 copy-start.2
  192.1 2.5 %fusion.3 = (f32[512,512]{1,0:T(8,128)}, f32[512,512]{1,0:T(8,128)}, f32[512,512]{1,0:T(8,128)}, f32[512,512]{1,0:T(8,128)}, f32[512,512]{1,0:T(8,128)}) fusion(bf16[2048,512]{1,0:T(8,128)(2,1)S(1)} %copy-done, bf16[1536,512]{1,0:T(8,128)(2,1)S(1)} %copy-done.1), kind=kLoop, calls=%fused_computation.7 | loop fusion | bytes 10485760 | tf_op jit(solution)/shard_map/slice | solution.py:790
  194.5 0.0 copy-done.3
  194.5 0.8 copy.31
  195.3 0.0 copy-done.2
  195.3 1.0 copy.32
Async XLA Ops:
  0.6 9.0 %copy-start.4 = (s32[2048]{0:T(1024)S(1)}, s32[2048]{0:T(1024)}, u32[]{:S(2)}) copy-start(s32[2048]{0:T(1024)} %param.15) | copy-start | bytes 24580
  3.6 7.4 %copy-start.5 = (s32[512]{0:T(512)}, s32[512]{0:T(512)S(1)}, u32[]{:S(2)}) copy-start(s32[512]{0:T(512)S(1)} %convert_add_fusion) | copy-start | bytes 6148
  189.0 3.0 %copy-start = (bf16[2048,512]{1,0:T(8,128)(2,1)S(1)}, bf16[2048,512]{1,0:T(8,128)(2,1)}, u32[]{:S(2)}) copy-start(bf16[2048,512]{1,0:T(8,128)(2,1)} %get-tuple-element.39) | copy-start | bytes 6291460
  189.1 3.0 %copy-start.1 = (bf16[1536,512]{1,0:T(8,128)(2,1)S(1)}, bf16[1536,512]{1,0:T(8,128)(2,1)}, u32[]{:S(2)}) copy-start(bf16[1536,512]{1,0:T(8,128)(2,1)} %get-tuple-element.38) | copy-start | bytes 4718596
  192.1 2.5 %copy-start.3 = (bf16[512,512]{1,0:T(8,128)(2,1)S(1)}, bf16[512,512]{1,0:T(8,128)(2,1)}, u32[]{:S(2)}) copy-start(bf16[512,512]{1,0:T(8,128)(2,1)} %get-tuple-element.56) | copy-start | bytes 1572868
  192.1 3.3 %copy-start.2 = (f32[512,512]{1,0:T(8,128)S(1)}, f32[512,512]{1,0:T(8,128)}, u32[]{:S(2)}) copy-start(f32[512,512]{1,0:T(8,128)} %get-tuple-element.57) | copy-start | bytes 3145732

commit v5 on v4

--- a/solution.py
+++ b/solution.py
@@ -518,6 +518,9 @@
     trade = Trade(rows, cols, update_away, update_home, update_send, update_recv)
     barrier = pltpu.get_barrier_semaphore()
     trade.greet(barrier)
+    update_away[...] = update_slots[...]
+    pl.semaphore_wait(barrier, rows * cols - 1)
+    trade.start()
 
     count_rows, width = nodes.shape
     extra = halo.shape[0]
@@ -531,16 +534,14 @@
     early_flat[2 * width : 3 * width, :] = low(scale * left_product(own, grad_hidden))
     early_flat[3 * width : 4 * width, :] = low(scale * left_product(aggregate[...], grad_hidden))
     pack(early_flat, early_own)
-    update_away[...] = update_slots[...]
-    pl.semaphore_wait(barrier, rows * cols - 1)
     early.begin()
-    trade.start()
     grad_aggregate[...] = low(right_product(grad_hidden, inner_weight[width:, :]))
     node_gradient[...] = grad_refined + right_product(grad_hidden, inner_weight[0:width, :])
     source_sums[...] = jnp.zeros_like(source_sums)
     target_sums[...] = jnp.zeros_like(target_sums)
     edge_sums[...] = jnp.zeros_like(edge_sums)
 
+    done = 0
     for number in range(edge_linear.shape[0] // block):
         here = pl.ds(number * block, block)
         picked = product(hot_rows(target_column[here, :], count_rows), grad_aggregate[...])
@@ -552,9 +553,9 @@
         )
         source_sums[...] += product(hot_columns(source_row[number], count_rows + extra), grad_edges)
         target_sums[...] += product(hot_columns(target_row[number], count_rows), grad_edges)
-        if number < early.steps:
-            early.advance(number)
-    done = min(edge_linear.shape[0] // block, early.steps)
+        if number == 1 or number == 3:
+            early.advance(done)
+            done += 1
 
     grad_sources = low(source_sums[...])
     grad_targets = low(target_sums[...])
@@ -598,16 +599,18 @@
         keep = jnp.where(inside[number], 1.0, 0.0).astype(jnp.bfloat16)
         landed[here, :] = landed[here, :] * keep
     node_gradient[...] += product(hot_columns(list_row[...], count_rows), landed[...])
-    trade.finish()
-    places = update_home.shape[0] * update_home.shape[1]
-    updated[...] = low(
-        refined[...].astype(jnp.float32) + product(hot_rows(slot_column[...], places), trade.rows())
-    )
     for step in range(late.steps):
         if done + step < early.steps:
             early.advance(done + step)
             if done + step == early.steps - 1:
                 unpack(early_out, early_sums)
+        if step == late.steps - 2:
+            trade.finish()
+            places = update_home.shape[0] * update_home.shape[1]
+            updated[...] = low(
+                refined[...].astype(jnp.float32)
+                + product(hot_rows(slot_column[...], places), trade.rows())
+            )
         late.advance(step)
     unpack(late_out, late_sums)
 

time: 197 us -> 184 us (0.934)
  Pallas kernels: 178 us -> 166 us
    pallas_call x1, Pallas kernels: 100 us -> 87.8 us  [local(): pl.pallas_call(functools.partial(backward_kernel, rows, cols, block, scal...]
where the time goes in v5:
time: 184 us
  Pallas kernels  166 us (90%)
  local copies, waits for them, and re-layouts  15.9 us (9%)
    pallas_call x1, Pallas kernels, local(): pl.pallas_call(functools.partial(backward_kernel, rows, cols, block, scal...  87.8 us
    pallas_call x1, Pallas kernels, local(): pl.pallas_call(functools.partial(forward_kernel, rows, cols, block), out_...  77.9 us

profile of v5, /device:TPU:0, one launch (start us, length us, event | category | flops | bytes accessed | tf_op | source)
XLA Modules:
  0.0 184.0 jit_solution(101329664465389794)
XLA Ops:
  0.6 0.0 copy-start.4
  0.6 1.3 broadcast_in_dim_reshape_squeeze.7.list_row
  1.9 1.0 fusion
  3.0 0.7 convert_add_fusion
  3.6 0.0 copy-start.5
  3.6 1.4 broadcast_in_dim_reshape_squeeze.8.list_column
  5.1 0.9 copy.23.slot_column
  5.9 1.7 copy.24.table_column
  7.6 2.0 %copy.26.target_column = s32[2048,1]{1,0:T(8,128)} copy(s32[2048,1]{0,1:T(1,128)} %bitcast.9) | data formatting | bytes 16384 | tf_op jit(solution)/shard_map/broadcast_in_dim | solution.py:654
  9.7 0.0 copy-done.4
  9.7 1.3 copy.25.source_column
  11.0 0.0 copy-done.5
  11.0 77.9 %shard_map.188 = (bf16[2048,512]{1,0:T(8,128)(2,1)}, bf16[2048,512]{1,0:T(8,128)(2,1)}, bf16[2048,512]{1,0:T(8,128)(2,1)}, bf16[512,512]{1,0:T(8,128)(2,1)}, f32...) custom-call(bf16[512,512]{1,0:T(8,128)(2,1)} %nodes.3, ...), custom_call_target="tpu_custom_call" | custom-call | flops 6442450944 | bytes 16777216 | tf_op jit(solution)/shard_map/pallas_call | solution.py:672
  88.9 87.8 %shard_map.189 = (f32[512,512]{1,0:T(8,128)}, bf16[512,512]{1,0:T(8,128)(2,1)}, bf16[2048,512]{1,0:T(8,128)(2,1)}, bf16[1536,512]{1,0:T(8,128)(2,1)}) custom-call(bf16[512,512]{1,0:T(8,128)(2,1)} %nodes.3, bf16[128,512]{1,0:T(8,128)(2,1)} %get-tuple-element.24.halo, bf16[512,512]{1,0:T(8,128)(2,1)} %cotangent.3, f32[512,512]{1,0:T(8,128)} %get-tuple-element.25.share_rows, ...), custom_call_target="tpu_custom_call" | custom-call | flops 8589934592 | bytes 25165824 | tf_op jit(solution)/shard_map/pallas_call | solution.py:727
  176.7 0.0 copy-start
  176.8 0.0 copy-start.1
  176.8 3.0 %slice.27 = f32[1024,512]{1,0:T(8,128)} slice(bf16[2048,512]{1,0:T(8,128)(2,1)} %get-tuple-element.39), slice={[1024:2048], [0:512]} | slice | bytes 4194304 | tf_op jit(solution)/shard_map/slice | solution.py:791
  179.7 0.0 copy-done
  179.8 0.0 copy-done.1
  179.8 0.0 copy-start.3
  179.8 0.0 copy-start.2
  179.8 2.5 %fusion.3 = (f32[512,512]{1,0:T(8,128)}, f32[512,512]{1,0:T(8,128)}, f32[512,512]{1,0:T(8,128)}, f32[512,512]{1,0:T(8,128)}, f32[512,512]{1,0:T(8,128)}) fusion(bf16[2048,512]{1,0:T(8,128)(2,1)S(1)} %copy-done, bf16[1536,512]{1,0:T(8,128)(2,1)S(1)} %copy-done.1), kind=kLoop, calls=%fused_computation.7 | loop fusion | bytes 10485760 | tf_op jit(solution)/shard_map/slice | solution.py:793
  182.2 0.0 copy-done.3
  182.2 0.8 copy.31
  183.0 0.0 copy-done.2
  183.0 1.0 copy.32
Async XLA Ops:
  0.6 9.0 %copy-start.4 = (s32[2048]{0:T(1024)S(1)}, s32[2048]{0:T(1024)}, u32[]{:S(2)}) copy-start(s32[2048]{0:T(1024)} %param.15) | copy-start | bytes 24580
  3.6 7.4 %copy-start.5 = (s32[512]{0:T(512)}, s32[512]{0:T(512)S(1)}, u32[]{:S(2)}) copy-start(s32[512]{0:T(512)S(1)} %convert_add_fusion) | copy-start | bytes 6148
  176.7 3.0 %copy-start = (bf16[2048,512]{1,0:T(8,128)(2,1)S(1)}, bf16[2048,512]{1,0:T(8,128)(2,1)}, u32[]{:S(2)}) copy-start(bf16[2048,512]{1,0:T(8,128)(2,1)} %get-tuple-element.39) | copy-start | bytes 6291460
  176.8 3.0 %copy-start.1 = (bf16[1536,512]{1,0:T(8,128)(2,1)S(1)}, bf16[1536,512]{1,0:T(8,128)(2,1)}, u32[]{:S(2)}) copy-start(bf16[1536,512]{1,0:T(8,128)(2,1)} %get-tuple-element.38) | copy-start | bytes 4718596
  179.8 2.5 %copy-start.3 = (bf16[512,512]{1,0:T(8,128)(2,1)S(1)}, bf16[512,512]{1,0:T(8,128)(2,1)}, u32[]{:S(2)}) copy-start(bf16[512,512]{1,0:T(8,128)(2,1)} %get-tuple-element.56) | copy-start | bytes 1572868
  179.8 3.3 %copy-start.2 = (f32[512,512]{1,0:T(8,128)S(1)}, f32[512,512]{1,0:T(8,128)}, u32[]{:S(2)}) copy-start(f32[512,512]{1,0:T(8,128)} %get-tuple-element.57) | copy-start | bytes 3145732
